TPU v7x, 128 devices: a whole 4x4x4 slice. The times are simulated.
128 devices in a mesh: role: 2 (over core), dev: 64 (over z, y, x).
Axes of the slice: x: 4, y: 4, z: 4, core: 2. Of those that a mesh axis runs over, the one named last changes fastest.
Arguments:
- layer_in: bfloat16 [16384, 4096], P(('role', 'dev')), may hold values from -24 to 24
- norm_gain: float32 [4096], replicated, may hold values from 0.1 to 1.9
- routes: int32 [16384, 4], P(('role', 'dev')), may hold values from 0 to 127, all different within a row; in each aligned block of 128 rows (0 to 127, 128 to 255, ...) at most 5 rows name the same one
- gate_weights: float32 [16384, 4], P(('role', 'dev')), may hold values from 0.05 to 1
- out_grad: bfloat16 [16384, 4096], P(('role', 'dev')), may hold values from -6 to 6
- expert_gate_up: bfloat16 [128, 4096, 1536], P(('role', 'dev')), may hold values from -0.09375 to 0.09375
- expert_down: bfloat16 [128, 768, 4096], P(('role', 'dev')), may hold values from -0.21875 to 0.21875
Outputs:
- layer_out: bfloat16 [16384, 4096], P(('role', 'dev'))
- input_grad: bfloat16 [16384, 4096], P(('role', 'dev'))
- gate_grad: float32 [16384, 4], P(('role', 'dev'))
- gain_grad: float32 [4096], P(('role', 'dev'))
Inputs may be any that keep to these rules, and one draw needn't show every extreme that they name: `routes`: each row names 4 different experts. Among the 128 rows of one device no expert is named more than 5 times, a bound that some block reaches.
All inputs are finite; a program needn't handle non-finite values.
Results may differ from a plain program's by a relative error of at most 0.0065.
Values may be sent and summed in bfloat16 or wider, within the bound.
No kernel may reach another device: no remote copies, remote signals or barrier semaphores. Data moves between devices by JAX's collectives and lax.ppermute only.
A program may use at most 192 MiB of HBM per device.

v0:
```python
import jax
import jax.numpy as jnp
from jax import lax
from jax.sharding import PartitionSpec as P

epsilon = 1e-06


def swish_parts(projected, hidden_units):
    gate_part = projected[:, :hidden_units]
    up_part = projected[:, hidden_units:]
    sigmoid_val = jax.nn.sigmoid(gate_part)
    active = gate_part * sigmoid_val
    return (gate_part, up_part, sigmoid_val, active)


def transposed(left, right):
    return lax.dot_general(
        left, right, (((1,), (1,)), ((), ())), preferred_element_type=jnp.float32
    )


def to_experts(buffer):
    moved = lax.all_to_all(buffer, ("role", "dev"), split_axis=0, concat_axis=0, tiled=True)
    return moved


def to_owners(buffer):
    moved = lax.all_to_all(buffer, ("role", "dev"), split_axis=0, concat_axis=0, tiled=True)
    return moved


def expert_forward(arrived, w_gate_up, w_down, hidden_units):
    projected = jnp.dot(arrived, w_gate_up, preferred_element_type=jnp.float32)
    gate_part, up_part, sigmoid_val, active = swish_parts(projected, hidden_units)
    hidden = (active * up_part).astype(jnp.bfloat16)
    expert_rows = jnp.dot(hidden, w_down, preferred_element_type=jnp.float32).astype(jnp.bfloat16)
    return (expert_rows, (gate_part, up_part, sigmoid_val, active))


def expert_backward(grad_rows, saved, w_gate_up, w_down):
    gate_part, up_part, sigmoid_val, active = saved
    hidden_grad = transposed(grad_rows, w_down)
    gate_grad_part = hidden_grad * up_part * sigmoid_val * (1.0 + gate_part * (1.0 - sigmoid_val))
    pre_grad = jnp.concatenate([gate_grad_part, hidden_grad * active], axis=-1).astype(jnp.bfloat16)
    return transposed(pre_grad, w_gate_up).astype(jnp.bfloat16)


def body(layer_in, norm_gain, routes, gate_weights, out_grad, expert_gate_up, expert_down):
    token_count, model_width = layer_in.shape
    top_count = routes.shape[1]
    peer_count = lax.axis_size(("role", "dev"))
    slot_count = token_count * top_count * 5 // (4 * peer_count)
    pair_count = token_count * top_count
    hidden_units = expert_down.shape[1]
    residual = layer_in.astype(jnp.float32)
    root_mean = jnp.sqrt(jnp.mean(residual * residual, axis=-1, keepdims=True) + epsilon)
    unit_rows = residual / root_mean
    normed = (unit_rows * norm_gain).astype(jnp.bfloat16)
    flat_routes = routes.reshape(-1)
    one_hot = (flat_routes[:, None] == jnp.arange(peer_count, dtype=jnp.int32)[None, :]).astype(
        jnp.int32
    )
    slot_of = jnp.sum((jnp.cumsum(one_hot, axis=0) - one_hot) * one_hot, axis=-1)
    position = flat_routes * slot_count + slot_of
    slot_table = jnp.full((peer_count * slot_count,), pair_count, jnp.int32)
    slot_table = slot_table.at[position].set(jnp.arange(pair_count, dtype=jnp.int32))
    token_table = jnp.where(slot_table < pair_count, slot_table // top_count, token_count)
    zero_row = jnp.zeros((1, model_width), jnp.bfloat16)
    send_rows = jnp.concatenate([normed, zero_row], axis=0)[token_table].reshape(
        peer_count, slot_count, model_width
    )
    grad_float = out_grad.astype(jnp.float32)
    scaled = (
        (gate_weights[..., None] * grad_float[:, None, :])
        .astype(jnp.bfloat16)
        .reshape(pair_count, model_width)
    )
    send_grads = jnp.concatenate([scaled, zero_row], axis=0)[slot_table].reshape(
        peer_count, slot_count, model_width
    )
    w_gate_up = expert_gate_up[0]
    w_down = expert_down[0]
    arrived = to_experts(send_rows).reshape(-1, model_width)
    expert_rows, saved = expert_forward(arrived, w_gate_up, w_down, hidden_units)
    returned = to_owners(expert_rows.reshape(peer_count, slot_count, model_width)).reshape(
        -1, model_width
    )[position]
    grad_rows = to_experts(send_grads).reshape(-1, model_width)
    back_rows = expert_backward(grad_rows, saved, w_gate_up, w_down)
    came_back = to_owners(back_rows.reshape(peer_count, slot_count, model_width)).reshape(
        -1, model_width
    )[position]
    outs_float = returned.astype(jnp.float32).reshape(token_count, top_count, model_width)
    routed_sum = jnp.sum(gate_weights[..., None] * outs_float, axis=1)
    layer_out = (residual + routed_sum).astype(jnp.bfloat16)
    gate_grad = jnp.sum(outs_float * grad_float[:, None, :], axis=-1)
    normed_grad = jnp.sum(
        came_back.astype(jnp.float32).reshape(token_count, top_count, model_width), axis=1
    )
    local_terms = jnp.sum(normed_grad * unit_rows, axis=0)
    share = model_width // peer_count
    whole = lax.psum(local_terms, ("role", "dev"))
    gain_grad = lax.dynamic_slice_in_dim(whole, lax.axis_index(("role", "dev")) * share, share, 0)
    scaled_gain = normed_grad * norm_gain
    input_grad = (
        grad_float
        + (scaled_gain - unit_rows * jnp.mean(scaled_gain * unit_rows, axis=-1, keepdims=True))
        / root_mean
    ).astype(jnp.bfloat16)
    return (layer_out, input_grad, gate_grad, gain_grad)


def solution(mesh):
    in_specs = (
        P(("role", "dev"), None),
        P(),
        P(("role", "dev"), None),
        P(("role", "dev"), None),
        P(("role", "dev"), None),
        P(("role", "dev"), None, None),
        P(("role", "dev"), None, None),
    )
    out_specs = (
        P(("role", "dev"), None),
        P(("role", "dev"), None),
        P(("role", "dev"), None),
        P(("role", "dev")),
    )
    return jax.shard_map(body, mesh=mesh, in_specs=in_specs, out_specs=out_specs, check_vma=False)
```

profile of v0, /device:TPU:1, one launch (start us, length us, event | category | flops | bytes accessed | tf_op | source)
XLA Modules:
  0.0 676.9 jit_solution(1441249705937705225)
XLA Ops:
  0.6 0.8 copy.21
  1.6 0.7 broadcast_multiply_fusion
  2.4 0.2 fusion.18
  2.8 0.1 copy.20
  3.0 0.2 fusion.17
  3.2 2.4 scatter_custom_fusion
  5.7 1.5 fusion.10
  7.3 0.5 copy-done.3
  7.8 1.6 multiply_convert_fusion.1
  9.4 5.4 gather_fusion
  14.8 8.4 %reshape.115 = bf16[128,5,4096]{2,1,0:T(8,128)(2,1)} reshape(bf16[640,4096]{1,0:T(8,128)(2,1)} %gather_fusion) | data formatting | bytes 10485760 | tf_op jit(solution)/shard_map/reshape | solution.py:70
  23.2 12.7 %all-to-all-start = ((bf16[128,5,4096]{2,1,0:T(8,128)(2,1)}), bf16[128,5,4096]{2,1,0:T(8,128)(2,1)}, u32[]{:S(2)}, u32[]{:S(2)}) async-start(bf16[128,5,4096]{2,1,0:T(8,128)(2,1)} %reshape.115), calls=%async_computation | async-start | bytes 16777216 | tf_op jit(solution)/shard_map/all_to_all | solution.py:24
  35.9 0.1 copy.19
  36.1 5.3 mul.126
  41.4 10.0 %mul.127 = f32[512,4096]{1,0:T(8,128)} reshape(f32[128,4,4096]{2,1,0:T(4,128)} %mul.126) | data formatting | bytes 16777216 | tf_op jit(solution)/shard_map/mul | solution.py:75
  51.5 4.6 multiply_convert_fusion
  56.0 2.3 concatenate.11
  58.3 14.4 %gather_fusion.2 = bf16[640,4096]{1,0:T(8,128)(2,1)} fusion(bf16[513,4096]{1,0:T(8,128)(2,1)} %concatenate.11, s32[1024]{0:T(1024)S(1)} %get-tuple-element.18), kind=kCustom, calls=%fused_computation.2 | custom fusion | bytes 10488320 | tf_op jit(solution)/shard_map/gather | solution.py:79
  72.8 8.3 %reshape.119 = bf16[128,5,4096]{2,1,0:T(8,128)(2,1)} reshape(bf16[640,4096]{1,0:T(8,128)(2,1)} %gather_fusion.2) | data formatting | bytes 10485760 | tf_op jit(solution)/shard_map/reshape | solution.py:79
  81.1 65.5 %all-to-all-done = bf16[128,5,4096]{2,1,0:T(8,128)(2,1)} async-done(((bf16[128,5,4096]{2,1,0:T(8,128)(2,1)}), bf16[128,5,4096]{2,1,0:T(8,128)(2,1)}, u32[]{:S(2)}, u32[]{:S(2)}) %all-to-all-start) | async-done | bytes 5242912 | tf_op jit(solution)/shard_map/all_to_all | solution.py:24
  146.6 13.3 %all-to-all-start.2 = ((bf16[128,5,4096]{2,1,0:T(8,128)(2,1)}), bf16[128,5,4096]{2,1,0:T(8,128)(2,1)}, u32[]{:S(2)}, u32[]{:S(2)}) async-start(bf16[128,5,4096]{2,1,0:T(8,128)(2,1)} %reshape.119), calls=%async_computation.2 | async-start | bytes 16777216 | tf_op jit(solution)/shard_map/all_to_all | solution.py:24
  160.0 8.7 %reshape.116 = bf16[640,4096]{1,0:T(8,128)(2,1)} reshape(bf16[128,5,4096]{2,1,0:T(8,128)(2,1)} %all-to-all-done) | data formatting | bytes 10485760 | tf_op jit(solution)/shard_map/reshape | solution.py:84
  168.7 14.1 %fusion.2 = f32[640,1536]{1,0:T(8,128)} fusion(bf16[640,4096]{1,0:T(8,128)(2,1)} %reshape.116, bf16[1,4096,1536]{2,1,0:T(8,128)(2,1)} %param.12), kind=kOutput, calls=%fused_computation.7 | convolution fusion | flops 8053063680 | bytes 21757952 | tf_op jit(solution)/shard_map/dot_general | solution.py:34
  182.8 87.9 %all-to-all-done.2 = bf16[128,5,4096]{2,1,0:T(8,128)(2,1)} async-done(((bf16[128,5,4096]{2,1,0:T(8,128)(2,1)}), bf16[128,5,4096]{2,1,0:T(8,128)(2,1)}, u32[]{:S(2)}, u32[]{:S(2)}) %all-to-all-start.2) | async-done | bytes 5242912 | tf_op jit(solution)/shard_map/all_to_all | solution.py:24
  270.7 8.8 %reshape.120 = bf16[640,4096]{1,0:T(8,128)(2,1)} reshape(bf16[128,5,4096]{2,1,0:T(8,128)(2,1)} %all-to-all-done.2) | data formatting | bytes 10485760 | tf_op jit(solution)/shard_map/reshape | solution.py:89
  279.5 10.1 %multiply_convert_fusion.3 = (bf16[640,768]{1,0:T(8,128)(2,1)S(1)}, bf16[640,768]{1,0:T(8,128)(2,1)S(1)}) fusion(f32[640,1536]{1,0:T(8,128)} %fusion.2, bf16[640,4096]{1,0:T(8,128)(2,1)} %reshape.120, bf16[1,768,4096]{2,1,0:T(8,128)(2,1)} %param.13), kind=kOutput, calls=%fused_computation.30 | convolution fusion | flops 4032921600 | bytes 17432576 | tf_op jit(solution)/shard_map/dot_general | solution.py:18
  289.7 17.4 %fusion.4 = bf16[640,4096]{1,0:T(8,128)(2,1)} fusion(bf16[1,4096,1536]{2,1,0:T(8,128)(2,1)} %param.12, bf16[640,768]{1,0:T(8,128)(2,1)S(1)} %get-tuple-element.13, bf16[640,768]{1,0:T(8,128)(2,1)S(1)} %get-tuple-element.12), kind=kOutput, calls=%fused_computation.12 | convolution fusion | flops 8059617280 | bytes 19791872 | tf_op jit(solution)/shard_map/dot_general | solution.py:18
  307.1 8.4 %reshape.121 = bf16[128,5,4096]{2,1,0:T(8,128)(2,1)} reshape(bf16[640,4096]{1,0:T(8,128)(2,1)} %fusion.4) | data formatting | bytes 10485760 | tf_op jit(solution)/shard_map/reshape | solution.py:91
  315.5 13.0 %all-to-all-start.3 = ((bf16[128,5,4096]{2,1,0:T(8,128)(2,1)}), bf16[128,5,4096]{2,1,0:T(8,128)(2,1)}, u32[]{:S(2)}, u32[]{:S(2)}) async-start(bf16[128,5,4096]{2,1,0:T(8,128)(2,1)} %reshape.121), calls=%async_computation.3 | async-start | bytes 16777216 | tf_op jit(solution)/shard_map/all_to_all | solution.py:29
  328.5 10.6 %convolution_convert_fusion = bf16[640,4096]{1,0:T(8,128)(2,1)} fusion(bf16[1,768,4096]{2,1,0:T(8,128)(2,1)} %param.13, f32[640,1536]{1,0:T(8,128)} %fusion.2), kind=kOutput, calls=%fused_computation.13 | convolution fusion | flops 4032102400 | bytes 15466496 | tf_op jit(solution)/shard_map/dot_general | solution.py:37
  339.1 8.4 %reshape.117 = bf16[128,5,4096]{2,1,0:T(8,128)(2,1)} reshape(bf16[640,4096]{1,0:T(8,128)(2,1)} %convolution_convert_fusion) | data formatting | bytes 10485760 | tf_op jit(solution)/shard_map/reshape | solution.py:86
  347.5 94.8 %all-to-all-done.3 = bf16[128,5,4096]{2,1,0:T(8,128)(2,1)} async-done(((bf16[128,5,4096]{2,1,0:T(8,128)(2,1)}), bf16[128,5,4096]{2,1,0:T(8,128)(2,1)}, u32[]{:S(2)}, u32[]{:S(2)}) %all-to-all-start.3) | async-done | bytes 5242912 | tf_op jit(solution)/shard_map/all_to_all | solution.py:29
  442.2 9.3 %all-to-all-start.1 = ((bf16[128,5,4096]{2,1,0:T(8,128)(2,1)}), bf16[128,5,4096]{2,1,0:T(8,128)(2,1)}, u32[]{:S(2)}, u32[]{:S(2)}) async-start(bf16[128,5,4096]{2,1,0:T(8,128)(2,1)} %reshape.117), calls=%async_computation.1 | async-start | bytes 16777216 | tf_op jit(solution)/shard_map/all_to_all | solution.py:29
  451.5 1.6 convert_element_type.63
  453.1 8.8 %reshape.122 = bf16[640,4096]{1,0:T(8,128)(2,1)} reshape(bf16[128,5,4096]{2,1,0:T(8,128)(2,1)} %all-to-all-done.3) | data formatting | bytes 10485760 | tf_op jit(solution)/shard_map/reshape | solution.py:91
  461.9 11.8 %gather_fusion.3 = bf16[512,4096]{1,0:T(8,128)(2,1)} fusion(bf16[640,4096]{1,0:T(8,128)(2,1)} %reshape.122, s32[1024]{0:T(1024)S(1)} %pad_clamp_fusion.1), kind=kCustom, calls=%fused_computation.3 | custom fusion | bytes 8390656 | tf_op jit(solution)/shard_map/gather | solution.py:91
  473.6 8.3 %reshape.124 = f32[128,4,4096]{2,1,0:T(4,128)} reshape(bf16[512,4096]{1,0:T(8,128)(2,1)} %gather_fusion.3) | data formatting | bytes 12582912 | tf_op jit(solution)/shard_map/convert_element_type | solution.py:99
  482.0 8.8 %reduce_sum.69 = f32[128,4096]{1,0:T(8,128)S(1)} reduce(f32[128,4,4096]{2,1,0:T(4,128)} %reshape.124, f32[]{:T(128)} %constant.16.clone.1), dimensions={1}, to_apply=%region_6.7 | reduce | flops 1572864 | bytes 10485764 | tf_op jit(solution)/shard_map/reduce_sum | solution.py:98
  490.8 0.7 multiply_reduce_fusion.2
  491.5 70.8 %all-to-all-done.1 = bf16[128,5,4096]{2,1,0:T(8,128)(2,1)} async-done(((bf16[128,5,4096]{2,1,0:T(8,128)(2,1)}), bf16[128,5,4096]{2,1,0:T(8,128)(2,1)}, u32[]{:S(2)}, u32[]{:S(2)}) %all-to-all-start.1) | async-done | bytes 5242912 | tf_op jit(solution)/shard_map/all_to_all | solution.py:29
  562.3 9.0 %reshape.118 = bf16[640,4096]{1,0:T(8,128)(2,1)} reshape(bf16[128,5,4096]{2,1,0:T(8,128)(2,1)} %all-to-all-done.1) | data formatting | bytes 10485760 | tf_op jit(solution)/shard_map/reshape | solution.py:86
  571.3 11.8 %gather_fusion.1 = bf16[512,4096]{1,0:T(8,128)(2,1)} fusion(bf16[640,4096]{1,0:T(8,128)(2,1)} %reshape.118, s32[1024]{0:T(1024)S(1)} %pad_clamp_fusion.1), kind=kCustom, calls=%fused_computation.1 | custom fusion | bytes 8390656 | tf_op jit(solution)/shard_map/gather | solution.py:86
  583.1 8.3 %reshape.123 = f32[128,4,4096]{2,1,0:T(4,128)} reshape(bf16[512,4096]{1,0:T(8,128)(2,1)} %gather_fusion.1) | data formatting | bytes 12582912 | tf_op jit(solution)/shard_map/convert_element_type | solution.py:94
  591.3 68.9 %psum.7 = f32[4096]{0:T(1024)S(1)} all-reduce(f32[4096]{0:T(1024)S(1)} %get-tuple-element.10), channel_id=1, replica_groups=mesh['role'=2,'dev'=64] {'role','dev'}, use_global_device_ids=true, to_apply=%region_10.11 | all-reduce | flops 4096 | bytes 32768 | tf_op jit(solution)/shard_map/psum | solution.py:103
  660.2 10.9 %multiply_reduce_fusion = (f32[128,4]{1,0:T(8,128)S(1)}, f32[128,4096]{1,0:T(8,128)}) fusion(f32[128,4,4096]{2,1,0:T(4,128)} %reshape.123, f32[128,4096]{1,0:T(8,128)} %convert_element_type.63, f32[128,4]{1,0:T(8,128)S(1)} %copy.19), kind=kLoop, calls=%fused_computation.9 | loop fusion | flops 7863808 | bytes 12587008 | tf_op jit(solution)/shard_map/reduce_sum | solution.py:97
  671.1 0.7 copy.26
  671.7 4.1 add_convert_fusion
  675.8 0.6 dynamic_slice.3
  (30 shorter events, 0.8 us)
Async XLA Ops:
  7.2 0.5 copy-start.3
  23.2 12.7 %copy-start.5 = (f32[128,4]{0,1:T(4,128)S(1)}, f32[128,4]{0,1:T(4,128)}, u32[]{:S(2)}) copy-start(f32[128,4]{0,1:T(4,128)} %param.10) | copy-start | bytes 6148
  23.2 12.9 %copy-start.1 = (bf16[128,4096]{1,0:T(8,128)(2,1)S(1)}, bf16[128,4096]{1,0:T(8,128)(2,1)}, u32[]{:S(2)}) copy-start(bf16[128,4096]{1,0:T(8,128)(2,1)} %param.11) | copy-start | bytes 3145732
  23.2 123.4 %all-to-all-start = ((bf16[128,5,4096]{2,1,0:T(8,128)(2,1)}), bf16[128,5,4096]{2,1,0:T(8,128)(2,1)}, u32[]{:S(2)}, u32[]{:S(2)}) async-start(bf16[128,5,4096]{2,1,0:T(8,128)(2,1)} %reshape.115), calls=%async_computation | async-start | bytes 16777216 | tf_op jit(solution)/shard_map/all_to_all | solution.py:24
  146.6 124.1 %all-to-all-start.2 = ((bf16[128,5,4096]{2,1,0:T(8,128)(2,1)}), bf16[128,5,4096]{2,1,0:T(8,128)(2,1)}, u32[]{:S(2)}, u32[]{:S(2)}) async-start(bf16[128,5,4096]{2,1,0:T(8,128)(2,1)} %reshape.119), calls=%async_computation.2 | async-start | bytes 16777216 | tf_op jit(solution)/shard_map/all_to_all | solution.py:24
  315.5 126.8 %all-to-all-start.3 = ((bf16[128,5,4096]{2,1,0:T(8,128)(2,1)}), bf16[128,5,4096]{2,1,0:T(8,128)(2,1)}, u32[]{:S(2)}, u32[]{:S(2)}) async-start(bf16[128,5,4096]{2,1,0:T(8,128)(2,1)} %reshape.121), calls=%async_computation.3 | async-start | bytes 16777216 | tf_op jit(solution)/shard_map/all_to_all | solution.py:29
  442.2 120.0 %all-to-all-start.1 = ((bf16[128,5,4096]{2,1,0:T(8,128)(2,1)}), bf16[128,5,4096]{2,1,0:T(8,128)(2,1)}, u32[]{:S(2)}, u32[]{:S(2)}) async-start(bf16[128,5,4096]{2,1,0:T(8,128)(2,1)} %reshape.117), calls=%async_computation.1 | async-start | bytes 16777216 | tf_op jit(solution)/shard_map/all_to_all | solution.py:29
  482.0 8.8 %copy-start = (bf16[128,4096]{1,0:T(8,128)(2,1)S(1)}, bf16[128,4096]{1,0:T(8,128)(2,1)}, u32[]{:S(2)}) copy-start(bf16[128,4096]{1,0:T(8,128)(2,1)} %param.7) | copy-start | bytes 3145732
  482.0 8.8 %copy-start.2 = (f32[4096]{0:T(1024)S(1)}, f32[4096]{0:T(1024)}, u32[]{:S(2)}) copy-start(f32[4096]{0:T(1024)} %param.8) | copy-start | bytes 49156
  482.0 8.8 %copy-start.4 = (f32[128]{0:T(128)S(1)}, f32[128]{0:T(128)}, u32[]{:S(2)}) copy-start(f32[128]{0:T(128)} %copy-done.3) | copy-start | bytes 1540
where the time goes:
time: 684 us; the launch traced here: 677 us
  waiting for transfers between devices  319 us (47%)
  local copies, waits for them, and re-layouts  152 us (22%)
  blocking collectives  68.9 us (10%)
  matrix products  52.3 us (8%)
  starting transfers between devices  48.3 us (7%)
  other arithmetic  34.9 us (5%)
    all_to_all x2, waiting for transfers between devices, to_owners(): lax.all_to_all(buffer, ('role', 'dev'), split_axis=0, concat_axis=0, tile...  166 us
    all_to_all x2, waiting for transfers between devices, to_experts(): lax.all_to_all(buffer, ('role', 'dev'), split_axis=0, concat_axis=0, tile...  153 us
    psum x1, blocking collectives, body(): whole = lax.psum(local_terms, ('role', 'dev'))  68.9 us
    dot_general x2, matrix products, transposed(): lax.dot_general(left, right, (((1,), (1,)), ((), ())), preferred_element_...  27.6 us
    all_to_all x2, starting transfers between devices, to_experts(): lax.all_to_all(buffer, ('role', 'dev'), split_axis=0, concat_axis=0, tile...  26 us
    all_to_all x2, starting transfers between devices, to_owners(): lax.all_to_all(buffer, ('role', 'dev'), split_axis=0, concat_axis=0, tile...  22.3 us
    mul x2, local copies, waits for them, and re-layouts, body(): gate_weights[..., None] * grad_float[:, None, :]  15.3 us
    gather x1, local copies, waits for them, and re-layouts, body(): jnp.concatenate([scaled, zero_row], axis=0)[slot_table]  14.4 us
  transfers between devices with their start and end apart: 4, of which 4 were waited for; matrix products, arithmetic and copies ran while one was open for 19% of the time, Pallas kernels for 0%

commit v1 on v0

v1 whole, which is shorter than its diff:
```python
import jax
import jax.numpy as jnp
from jax import lax
from jax.experimental import pallas as pl
from jax.experimental.pallas import tpu as pltpu
from jax.sharding import PartitionSpec as P

AXES = ("role", "dev")
EPSILON = 1e-06
LANES = 128
GROUP = 16
EXTRA = 8
F32 = jnp.float32
BF16 = jnp.bfloat16
VMEM = pl.BlockSpec(memory_space=pltpu.VMEM)
SMEM = pl.BlockSpec(memory_space=pltpu.SMEM)
PARAMS = pltpu.CompilerParams(vmem_limit_bytes=40 * 1024 * 1024)


def zero_fill(ref):
    def one(i, carry):
        ref[i] = jnp.zeros(ref.shape[1:], ref.dtype)
        return carry

    lax.fori_loop(0, ref.shape[0], one, 0)


def columns_of(ref, first, piece):
    return ref[pl.ds(first, GROUP), piece * LANES : (piece + 1) * LANES].astype(F32)


def strip(group, piece, pieces):
    return pl.ds(group * GROUP * pieces + piece, GROUP, stride=pieces)


def token_rows(token, pieces):
    return pl.ds(pl.multiple_of(token * pieces, pieces), pieces)


def slot_rows(slot, pieces):
    return pl.ds(pl.multiple_of(slot * pieces, pieces), pieces)


def send_rows_kernel(routes, layer_in, gain, out, place, rows, count):
    tokens, width = layer_in.shape
    pieces = width // LANES
    top = routes.shape[0]

    def clear(i, carry):
        count[i] = 0
        return carry

    lax.fori_loop(0, count.shape[0], clear, 0)
    zero_fill(out)

    def normalise(group, carry):
        first = pl.multiple_of(group * GROUP, GROUP)
        square = jnp.zeros((GROUP, LANES), F32)
        for piece in range(pieces):
            x = columns_of(layer_in, first, piece)
            square = square + x * x
        root_mean = jnp.sqrt(jnp.sum(square, axis=-1, keepdims=True) / width + EPSILON)
        inverse = 1.0 / root_mean
        for piece in range(pieces):
            unit = columns_of(layer_in, first, piece) * inverse
            rows[strip(group, piece, pieces), :] = (
                unit * gain[:, piece * LANES : (piece + 1) * LANES]
            )
        return carry

    lax.fori_loop(0, tokens // GROUP, normalise, 0)

    def place_token(token, carry):
        row = rows[token_rows(token, pieces), :].astype(BF16)
        for k in range(top):
            expert = routes[k, token]
            slot = count[expert]
            count[expert] = slot + 1
            place[k, token] = expert * 8 + slot
            out[expert, slot_rows(slot, pieces), :] = row
        return carry

    lax.fori_loop(0, tokens, place_token, 0)


def send_grads_kernel(place, weights, out_grad, out, rows):
    tokens, width = out_grad.shape
    pieces = width // LANES
    top = place.shape[0]
    zero_fill(out)

    def spread(group, carry):
        first = pl.multiple_of(group * GROUP, GROUP)
        for piece in range(pieces):
            rows[strip(group, piece, pieces), :] = columns_of(out_grad, first, piece)
        return carry

    lax.fori_loop(0, tokens // GROUP, spread, 0)

    def place_token(token, carry):
        row = rows[token_rows(token, pieces), :]
        for k in range(top):
            where = place[k, token]
            out[where // 8, slot_rows(where % 8, pieces), :] = (row * weights[k, token]).astype(BF16)
        return carry

    lax.fori_loop(0, tokens, place_token, 0)


def outputs_kernel(place, weights, layer_in, out_grad, returned, layer_out, gate_grad, rows, sums, dots):
    tokens, width = out_grad.shape
    pieces = width // LANES
    top = place.shape[0]

    def spread(group, carry):
        first = pl.multiple_of(group * GROUP, GROUP)
        for piece in range(pieces):
            rows[strip(group, piece, pieces), :] = columns_of(out_grad, first, piece)
        return carry

    lax.fori_loop(0, tokens // GROUP, spread, 0)

    def combine(token, carry):
        grad = rows[token_rows(token, pieces), :]
        total = jnp.zeros((pieces, LANES), F32)
        for k in range(top):
            where = place[k, token]
            row = returned[where // 8, slot_rows(where % 8, pieces), :].astype(F32)
            total = total + weights[k, token] * row
            dots[k, pl.ds(token, 1), :] = jnp.sum(row * grad, axis=0, keepdims=True)
        sums[token_rows(token, pieces), :] = total
        return carry

    lax.fori_loop(0, tokens, combine, 0)
    for k in range(top):
        gate_grad[k : k + 1, :] = jnp.sum(dots[k].T, axis=0, keepdims=True)

    def finish(group, carry):
        first = pl.multiple_of(group * GROUP, GROUP)
        for piece in range(pieces):
            x = columns_of(layer_in, first, piece)
            layer_out[pl.ds(first, GROUP), piece * LANES : (piece + 1) * LANES] = (
                x + sums[strip(group, piece, pieces), :]
            ).astype(BF16)
        return carry

    lax.fori_loop(0, tokens // GROUP, finish, 0)


def input_grad_kernel(place, layer_in, gain, out_grad, returned, input_grad, gain_grad, sums):
    tokens, width = out_grad.shape
    pieces = width // LANES
    top = place.shape[0]
    peers = returned.shape[0]
    body_rows = returned.shape[1] - EXTRA

    def combine(token, carry):
        total = jnp.zeros((pieces, LANES), F32)
        for k in range(top):
            where = place[k, token]
            total = total + returned[where // 8, slot_rows(where % 8, pieces), :].astype(F32)
        sums[token_rows(token, pieces), :] = total
        return carry

    lax.fori_loop(0, tokens, combine, 0)

    def finish(group, carry):
        first = pl.multiple_of(group * GROUP, GROUP)
        square = jnp.zeros((GROUP, LANES), F32)
        along = jnp.zeros((GROUP, LANES), F32)
        for piece in range(pieces):
            x = columns_of(layer_in, first, piece)
            q = sums[strip(group, piece, pieces), :] * gain[:, piece * LANES : (piece + 1) * LANES]
            square = square + x * x
            along = along + q * x
        inverse = 1.0 / jnp.sqrt(jnp.sum(square, axis=-1, keepdims=True) / width + EPSILON)
        mean = jnp.sum(along, axis=-1, keepdims=True) * inverse / width
        for piece in range(pieces):
            cut = slice(piece * LANES, (piece + 1) * LANES)
            unit = columns_of(layer_in, first, piece) * inverse
            q = sums[strip(group, piece, pieces), :] * gain[:, cut]
            input_grad[pl.ds(first, GROUP), cut] = (
                columns_of(out_grad, first, piece) + (q - unit * mean) * inverse
            ).astype(BF16)
        return carry

    lax.fori_loop(0, tokens // GROUP, finish, 0)

    def add_peer(peer, total):
        return total + returned[peer, body_rows : body_rows + EXTRA, :].astype(F32)

    gain_grad[...] = lax.fori_loop(0, peers, add_peer, jnp.zeros((EXTRA, LANES), F32))


def transposed(left, right):
    return lax.dot_general(left, right, (((1,), (1,)), ((), ())), preferred_element_type=F32)


def exchange(buffer):
    return lax.all_to_all(buffer, AXES, split_axis=0, concat_axis=0, tiled=True)


def three_parts(values):
    high = lax.reduce_precision(values, 8, 7)
    middle = lax.reduce_precision(values - high, 8, 7)
    low = values - high - middle
    return high.astype(BF16), middle.astype(BF16), low.astype(BF16)


def body(layer_in, norm_gain, routes, gate_weights, out_grad, expert_gate_up, expert_down):
    tokens, width = layer_in.shape
    top = routes.shape[1]
    peers = lax.axis_size(AXES)
    slots = tokens * top * 5 // (4 * peers)
    pieces = width // LANES
    hidden_units = expert_down.shape[1]
    row_count = peers * slots
    block = (peers, slots * pieces, LANES)
    gain = norm_gain.reshape(1, width)
    by_choice = routes.T
    weights = gate_weights.T
    token_scratch = pltpu.VMEM((tokens * pieces, LANES), F32)

    send_rows, place = pl.pallas_call(
        send_rows_kernel,
        out_shape=(
            jax.ShapeDtypeStruct(block, BF16),
            jax.ShapeDtypeStruct((top, tokens), jnp.int32),
        ),
        in_specs=[SMEM, VMEM, VMEM],
        out_specs=(VMEM, SMEM),
        scratch_shapes=[token_scratch, pltpu.SMEM((peers,), jnp.int32)],
        compiler_params=PARAMS,
        name="send_rows",
    )(by_choice, layer_in, gain)
    arrived = exchange(send_rows).reshape(row_count, pieces, LANES).reshape(row_count, width)

    send_grads = pl.pallas_call(
        send_grads_kernel,
        out_shape=jax.ShapeDtypeStruct(block, BF16),
        in_specs=[SMEM, SMEM, VMEM],
        out_specs=VMEM,
        scratch_shapes=[token_scratch],
        compiler_params=PARAMS,
        name="send_grads",
    )(place, weights, out_grad)
    grad_rows = exchange(send_grads).reshape(row_count, pieces, LANES).reshape(row_count, width)

    w_gate_up = expert_gate_up[0]
    w_down = expert_down[0]
    projected = jnp.dot(arrived, w_gate_up, preferred_element_type=F32)
    g = projected[:, :hidden_units]
    u = projected[:, hidden_units:]
    s = jax.nn.sigmoid(g)
    active = g * s
    hidden = (active * u).astype(BF16)
    expert_rows = jnp.dot(hidden, w_down, preferred_element_type=F32).astype(BF16)
    returned = exchange(expert_rows.reshape(row_count, pieces, LANES).reshape(block))

    hidden_grad = transposed(grad_rows, w_down)
    gate_part = hidden_grad * u * s * (1.0 + g * (1.0 - s))
    pre_grad = jnp.concatenate([gate_part, hidden_grad * active], axis=-1).astype(BF16)
    back_rows = transposed(pre_grad, w_gate_up).astype(BF16)
    terms = jnp.sum(back_rows.astype(F32) * arrived.astype(F32), axis=0) / norm_gain
    share = width // peers
    parts = jnp.concatenate([p.reshape(peers, share) for p in three_parts(terms)], axis=-1)
    parts = jnp.pad(parts[:, None, :], ((0, 0), (0, EXTRA - 1), (0, LANES - 3 * share)))
    send_back = jnp.concatenate(
        [back_rows.reshape(row_count, pieces, LANES).reshape(block), parts], axis=1
    )
    came_back = exchange(send_back)

    layer_out, gate_grad = pl.pallas_call(
        outputs_kernel,
        out_shape=(
            jax.ShapeDtypeStruct((tokens, width), BF16),
            jax.ShapeDtypeStruct((top, tokens), F32),
        ),
        in_specs=[SMEM, SMEM, VMEM, VMEM, VMEM],
        out_specs=(VMEM, VMEM),
        scratch_shapes=[token_scratch, token_scratch, pltpu.VMEM((top, tokens, LANES), F32)],
        compiler_params=PARAMS,
        name="outputs",
    )(place, weights, layer_in, out_grad, returned)

    input_grad, gain_sums = pl.pallas_call(
        input_grad_kernel,
        out_shape=(
            jax.ShapeDtypeStruct((tokens, width), BF16),
            jax.ShapeDtypeStruct((EXTRA, LANES), F32),
        ),
        in_specs=[SMEM, VMEM, VMEM, VMEM, VMEM],
        out_specs=(VMEM, VMEM),
        scratch_shapes=[token_scratch],
        compiler_params=PARAMS,
        name="input_grad",
    )(place, layer_in, gain, out_grad, came_back)
    gain_grad = jnp.sum(gain_sums[0, : 3 * share].reshape(3, share), axis=0)
    return (layer_out, input_grad, gate_grad.T, gain_grad)


def solution(mesh):
    split = P(AXES, None)
    in_specs = (split, P(), split, split, split, P(AXES, None, None), P(AXES, None, None))
    out_specs = (split, split, split, P(AXES))
    return jax.shard_map(body, mesh=mesh, in_specs=in_specs, out_specs=out_specs, check_vma=False)
```

time: 684 us -> 345 us (0.50)
  waiting for transfers between devices: 319 us -> 151 us
  local copies, waits for them, and re-layouts: 152 us -> 45.4 us
  blocking collectives: 68.9 us -> 0 us
  Pallas kernels: 0 us -> 40.4 us
  other arithmetic: 34.9 us -> 5.96 us
    all_to_all x4, waiting for transfers between devices: 319 us -> 151 us  [exchange(): return lax.all_to_all(buffer, AXES, split_axis=0, concat_axis=0, tiled=True)]
    psum x1 -> x0, blocking collectives: 68.9 us -> none  [body(): whole = lax.psum(local_terms, ('role', 'dev'))]
    reshape x8 -> x3, local copies, waits for them, and re-layouts: 68.8 us -> 0.25 us  [body(): p.reshape(peers, share)]
    gather x4 -> x0, local copies, waits for them, and re-layouts: 43.3 us -> none  [the longest x1 14.4 us: body(): jnp.concatenate([scaled, zero_row], axis=0)[slot_table]]
    pallas_call x0 -> x4, Pallas kernels: none -> 40.4 us  [the longest x1 12.2 us: body(): pl.pallas_call(outputs_kernel, out_shape=(jax.ShapeDtypeStruct((tokens, w...]
    another operation x3 -> x5, local copies, waits for them, and re-layouts: 0.03 us -> 35.8 us  [the longest x1 9 us: body(): exchange(send_rows).reshape(row_count, pieces, LANES)]
    reduce_sum x5 -> x1, other arithmetic: 22.1 us -> 0.53 us  [body(): gain_grad = jnp.sum(gain_sums[0, :3 * share].reshape(3, share), axis=0)]
    convert_element_type x2 -> x0, local copies, waits for them, and re-layouts: 16.6 us -> none  [the longest x1 8.33 us: body(): came_back.astype(jnp.float32).reshape(token_count, top_count, model_width)]
  transfers between devices with their start and end apart: 4 -> 4, of which waited for: 4 -> 4; matrix products, arithmetic and copies ran while one was open for 19% -> 26% of each run, Pallas kernels for 0% -> 6%
where the time goes in v1:
time: 345 us; the launch traced here: 339 us
  waiting for transfers between devices  151 us (44%)
  starting transfers between devices  49.3 us (14%)
  matrix products  46.4 us (13%)
  local copies, waits for them, and re-layouts  45.4 us (13%)
  Pallas kernels  40.4 us (12%)
  other arithmetic  5.96 us (2%)
    all_to_all x4, waiting for transfers between devices, exchange(): return lax.all_to_all(buffer, AXES, split_axis=0, concat_axis=0, tiled=True)  151 us
    all_to_all x4, starting transfers between devices, exchange(): return lax.all_to_all(buffer, AXES, split_axis=0, concat_axis=0, tiled=True)  49.3 us
    dot_general x2, matrix products, transposed(): lax.dot_general(left, right, (((1,), (1,)), ((), ())), preferred_element_...  27.8 us
    dot_general x1, matrix products, body(): projected = jnp.dot(arrived, w_gate_up, preferred_element_type=F32)  12.5 us
    pallas_call x1, Pallas kernels, body(): pl.pallas_call(outputs_kernel, out_shape=(jax.ShapeDtypeStruct((tokens, w...  12.2 us
    pallas_call x1, Pallas kernels, body(): pl.pallas_call(input_grad_kernel, out_shape=(jax.ShapeDtypeStruct((tokens...  12 us
    unnamed x28, local copies, waits for them, and re-layouts  9.26 us
    another operation x1, local copies, waits for them, and re-layouts, body(): exchange(send_rows).reshape(row_count, pieces, LANES)  9 us
  transfers between devices with their start and end apart: 4, of which 4 were waited for; matrix products, arithmetic and copies ran while one was open for 26% of the time, Pallas kernels for 6%

profile of v1, /device:TPU:1, one launch (start us, length us, event | category | flops | bytes accessed | tf_op | source)
XLA Modules:
  0.0 339.1 jit_solution(5248113006810907758)
XLA Ops:
  0.6 0.0 copy-start.1
  0.6 1.2 copy-done.1
  1.9 0.7 copy-done.5
  2.6 0.7 copy-done.8
  3.3 8.5 %send_rows.1 = (bf16[128,160,128]{2,1,0:T(8,128)(2,1)S(1)}, s32[4,128]{1,0:T(4,128)S(1)}) custom-call(s32[4,128]{1,0:T(4,128)S(1)} %bitcast.28, bf16[128,4096]{1,0:T(8,128)(2,1)S(1)} %copy-done.1, f32[1,4096]{1,0:T(1,128)S(1)} %bitcast.24), custom_call_target="tpu_custom_call" | custom-call | tf_op jit(solution)/shard_map/send_rows/pallas_call | solution.py:224
  11.7 0.0 copy-start.4
  11.8 2.3 copy-done.4
  14.1 11.9 %all-to-all-start = ((bf16[128,160,128]{2,1,0:T(8,128)(2,1)}), bf16[128,160,128]{2,1,0:T(8,128)(2,1)}, u32[]{:S(2)}, u32[]{:S(2)}) async-start(bf16[128,160,128]{2,1,0:T(8,128)(2,1)} %copy-done.4), calls=%async_computation | async-start | bytes 10485760 | tf_op jit(solution)/shard_map/all_to_all | solution.py:200
  26.0 0.0 copy-done.3
  26.0 0.0 copy-done.7
  26.0 7.7 %send_grads.1 = bf16[128,160,128]{2,1,0:T(8,128)(2,1)S(1)} custom-call(s32[4,128]{1,0:T(4,128)S(1)} %get-tuple-element.10.place, f32[4,128]{1,0:T(4,128)S(1)} %bitcast.26, bf16[128,4096]{1,0:T(8,128)(2,1)S(1)} %copy-done.3), custom_call_target="tpu_custom_call" | custom-call | tf_op jit(solution)/shard_map/send_grads/pallas_call | solution.py:238
  33.7 0.0 copy-start
  33.7 2.4 copy-done
  36.1 54.8 %all-to-all-done = bf16[128,160,128]{2,1,0:T(8,128)(2,1)} async-done(((bf16[128,160,128]{2,1,0:T(8,128)(2,1)}), bf16[128,160,128]{2,1,0:T(8,128)(2,1)}, u32[]{:S(2)}, u32[]{:S(2)}) %all-to-all-start) | async-done | bytes 5242912 | tf_op jit(solution)/shard_map/all_to_all | solution.py:200
  90.9 12.4 %all-to-all-start.2 = ((bf16[128,160,128]{2,1,0:T(8,128)(2,1)}), bf16[128,160,128]{2,1,0:T(8,128)(2,1)}, u32[]{:S(2)}, u32[]{:S(2)}) async-start(bf16[128,160,128]{2,1,0:T(8,128)(2,1)} %copy-done), calls=%async_computation.2 | async-start | bytes 10485760 | tf_op jit(solution)/shard_map/all_to_all | solution.py:200
  103.3 0.0 slice-start.2
  103.4 9.0 %reshape_reshape.12 = bf16[640,4096]{1,0:T(8,128)(2,1)} reshape(bf16[128,160,128]{2,1,0:T(8,128)(2,1)} %all-to-all-done) | data formatting | bytes 10485760 | tf_op jit(solution)/shard_map/reshape;reshape | solution.py:236
  112.4 12.5 %fusion.2 = f32[640,1536]{1,0:T(8,128)S(1)} fusion(bf16[640,4096]{1,0:T(8,128)(2,1)} %reshape_reshape.12, bf16[1,4096,1536]{2,1,0:T(8,128)(2,1)} %param.12), kind=kOutput, calls=%fused_computation.2 | convolution fusion | flops 8053063680 | bytes 21757952 | tf_op jit(solution)/shard_map/dot_general | solution.py:251
  124.9 0.0 copy-start.9
  124.9 1.9 copy-done.9
  126.8 0.0 slice-done.2
  126.8 0.0 slice-done.3
  126.8 6.1 %convolution_convert_fusion = bf16[640,4096]{1,0:T(8,128)(2,1)} fusion(bf16[1,768,4096]{2,1,0:T(8,128)(2,1)S(1)} %bitcast.32, f32[640,1536]{1,0:T(8,128)S(1)} %fusion.2), kind=kOutput, calls=%fused_computation.8 | convolution fusion | flops 4032102400 | bytes 15466496 | tf_op jit(solution)/shard_map/dot_general | solution.py:257
  132.9 8.9 %reshape_reshape.13 = bf16[128,160,128]{2,1,0:T(8,128)(2,1)} reshape(bf16[640,4096]{1,0:T(8,128)(2,1)} %convolution_convert_fusion) | data formatting | bytes 10485760 | tf_op jit(solution)/shard_map/reshape;reshape | solution.py:258
  141.8 26.4 %all-to-all-done.2 = bf16[128,160,128]{2,1,0:T(8,128)(2,1)} async-done(((bf16[128,160,128]{2,1,0:T(8,128)(2,1)}), bf16[128,160,128]{2,1,0:T(8,128)(2,1)}, u32[]{:S(2)}, u32[]{:S(2)}) %all-to-all-start.2) | async-done | bytes 5242912 | tf_op jit(solution)/shard_map/all_to_all | solution.py:200
  168.2 12.5 %all-to-all-start.1 = ((bf16[128,160,128]{2,1,0:T(8,128)(2,1)}), bf16[128,160,128]{2,1,0:T(8,128)(2,1)}, u32[]{:S(2)}, u32[]{:S(2)}) async-start(bf16[128,160,128]{2,1,0:T(8,128)(2,1)} %reshape_reshape.13), calls=%async_computation.1 | async-start | bytes 10485760 | tf_op jit(solution)/shard_map/all_to_all | solution.py:200
  180.7 0.0 slice-start
  180.7 8.9 %reshape_reshape.14 = bf16[640,4096]{1,0:T(8,128)(2,1)} reshape(bf16[128,160,128]{2,1,0:T(8,128)(2,1)} %all-to-all-done.2) | data formatting | bytes 10485760 | tf_op jit(solution)/shard_map/reshape;reshape | solution.py:247
  189.6 10.3 %multiply_convert_fusion.1 = (bf16[640,768]{1,0:T(8,128)(2,1)S(1)}, bf16[640,768]{1,0:T(8,128)(2,1)S(1)}) fusion(f32[640,1536]{1,0:T(8,128)} %copy-done.9, bf16[640,4096]{1,0:T(8,128)(2,1)} %reshape_reshape.14, bf16[1,768,4096]{2,1,0:T(8,128)(2,1)} %param.13), kind=kOutput, calls=%fused_computation.17 | convolution fusion | flops 4032921600 | bytes 17432576 | tf_op jit(solution)/shard_map/dot_general | solution.py:196
  199.9 0.0 slice-done
  200.0 0.0 slice-done.1
  200.0 0.0 copy-start.6
  200.0 17.5 %multiply_reduce_fusion = (f32[4096]{0:T(1024)S(1)}, bf16[640,4096]{1,0:T(8,128)(2,1)}) fusion(bf16[640,4096]{1,0:T(8,128)(2,1)S(1)} %bitcast.30, bf16[1,4096,1536]{2,1,0:T(8,128)(2,1)} %param.12, bf16[640,768]{1,0:T(8,128)(2,1)S(1)} %get-tuple-element.17, bf16[640,768]{1,0:T(8,128)(2,1)S(1)} %get-tuple-element.16), kind=kOutput, calls=%fused_computation.6 | convolution fusion | flops 8070098944 | bytes 25051136 | tf_op jit(solution)/shard_map/dot_general | solution.py:196
  217.5 0.0 copy-done.6
  217.5 0.1 reshape.21
  217.6 0.1 reshape.22
  217.6 0.1 reshape.23
  217.7 0.1 maximum_bitcast_fusion
  217.8 0.1 copy.12
  217.9 8.9 %reshape_reshape.15 = bf16[128,160,128]{2,1,0:T(8,128)(2,1)} reshape(bf16[640,4096]{1,0:T(8,128)(2,1)} %get-tuple-element.22) | data formatting | bytes 10485760 | tf_op jit(solution)/shard_map/reshape;reshape | solution.py:269
  226.8 5.3 %fusion.11 = bf16[128,168,128]{2,1,0:T(8,128)(2,1)} fusion(bf16[128,1,96]{2,1,0:T(2,128)(2,1)S(1)} %copy.12, bf16[128,160,128]{2,1,0:T(8,128)(2,1)} %reshape_reshape.15), kind=kLoop, calls=%fused_computation.12 | loop fusion | flops 16515072 | bytes 10772480 | tf_op jit(solution)/shard_map/concatenate | solution.py:268
  232.1 13.5 %all-to-all-done.1.returned = bf16[128,160,128]{2,1,0:T(8,128)(2,1)} async-done(((bf16[128,160,128]{2,1,0:T(8,128)(2,1)}), bf16[128,160,128]{2,1,0:T(8,128)(2,1)}, u32[]{:S(2)}, u32[]{:S(2)}) %all-to-all-start.1) | async-done | bytes 5242912 | tf_op jit(solution)/shard_map/all_to_all | solution.py:200
  245.6 12.5 %all-to-all-start.3 = ((bf16[128,168,128]{2,1,0:T(8,128)(2,1)}), bf16[128,168,128]{2,1,0:T(8,128)(2,1)}, u32[]{:S(2)}, u32[]{:S(2)}) async-start(bf16[128,168,128]{2,1,0:T(8,128)(2,1)} %fusion.11), calls=%async_computation.3 | async-start | bytes 11010048 | tf_op jit(solution)/shard_map/all_to_all | solution.py:200
  258.1 12.2 %outputs.1 = (bf16[128,4096]{1,0:T(8,128)(2,1)}, f32[4,128]{1,0:T(4,128)}) custom-call(s32[4,128]{1,0:T(4,128)S(1)} %get-tuple-element.10.place, f32[4,128]{1,0:T(4,128)S(1)} %bitcast.27, bf16[128,4096]{1,0:T(8,128)(2,1)S(1)} %copy-done.2, bf16[128,4096]{1,0:T(8,128)(2,1)S(1)} %copy-done.3, bf16[128,160,128]{2,1,0:T(8,128)(2,1)} %all-to-all-done.1.returned), custom_call_target="tpu_custom_call" | custom-call | tf_op jit(solution)/shard_map/outputs/pallas_call | solution.py:273
  270.3 56.2 %all-to-all-done.3.returned = bf16[128,168,128]{2,1,0:T(8,128)(2,1)} async-done(((bf16[128,168,128]{2,1,0:T(8,128)(2,1)}), bf16[128,168,128]{2,1,0:T(8,128)(2,1)}, u32[]{:S(2)}, u32[]{:S(2)}) %all-to-all-start.3) | async-done | bytes 5505056 | tf_op jit(solution)/shard_map/all_to_all | solution.py:200
  326.5 12.0 %input_grad.1 = (bf16[128,4096]{1,0:T(8,128)(2,1)}, f32[8,128]{1,0:T(8,128)S(1)}) custom-call(s32[4,128]{1,0:T(4,128)S(1)} %get-tuple-element.10.place, bf16[128,4096]{1,0:T(8,128)(2,1)S(1)} %copy-done.2, f32[1,4096]{1,0:T(1,128)S(1)} %bitcast.25, bf16[128,4096]{1,0:T(8,128)(2,1)S(1)} %copy-done.3, bf16[128,168,128]{2,1,0:T(8,128)(2,1)} %all-to-all-done.3.returned), custom_call_target="tpu_custom_call" | custom-call | tf_op jit(solution)/shard_map/input_grad/pallas_call | solution.py:286
  338.5 0.1 reshape_squeeze.3
  338.5 0.5 reduce_sum.19
  (12 shorter events, 0.0 us)
Async XLA Ops:
  0.6 1.2 copy-start.1
  1.9 0.7 copy-start.5
  2.6 0.7 copy-start.8
  11.7 2.3 copy-start.4
  14.1 11.9 %copy-start.3 = (bf16[128,4096]{1,0:T(8,128)(2,1)S(1)}, bf16[128,4096]{1,0:T(8,128)(2,1)}, u32[]{:S(2)}) copy-start(bf16[128,4096]{1,0:T(8,128)(2,1)} %out_grad.5) | copy-start | bytes 3145732
  14.1 11.9 %copy-start.7 = (f32[128,4]{0,1:T(4,128)S(1)}, f32[128,4]{0,1:T(4,128)}, u32[]{:S(2)}) copy-start(f32[128,4]{0,1:T(4,128)} %param.10) | copy-start | bytes 6148
  14.1 76.8 %all-to-all-start = ((bf16[128,160,128]{2,1,0:T(8,128)(2,1)}), bf16[128,160,128]{2,1,0:T(8,128)(2,1)}, u32[]{:S(2)}, u32[]{:S(2)}) async-start(bf16[128,160,128]{2,1,0:T(8,128)(2,1)} %copy-done.4), calls=%async_computation | async-start | bytes 10485760 | tf_op jit(solution)/shard_map/all_to_all | solution.py:200
  33.7 2.4 copy-start
  90.9 77.4 %all-to-all-start.2 = ((bf16[128,160,128]{2,1,0:T(8,128)(2,1)}), bf16[128,160,128]{2,1,0:T(8,128)(2,1)}, u32[]{:S(2)}, u32[]{:S(2)}) async-start(bf16[128,160,128]{2,1,0:T(8,128)(2,1)} %copy-done), calls=%async_computation.2 | async-start | bytes 10485760 | tf_op jit(solution)/shard_map/all_to_all | solution.py:200
  103.3 23.5 %slice-start.2 = ((s8[6291456]{0:T(1024)(128)(4,1)}), s8[2097152]{0:T(1024)(128)(4,1)S(1)}, s32[]{:S(2)}) async-start(s8[6291456]{0:T(1024)(128)(4,1)} %bitcast.31), calls=%async_computation.6 | async-start | bytes 4194304
  112.4 14.5 %slice-start.3 = ((s8[6291456]{0:T(1024)(128)(4,1)}), s8[4194304]{0:T(1024)(128)(4,1)S(1)}, s32[]{:S(2)}) async-start(s8[6291456]{0:T(1024)(128)(4,1)} %bitcast.31), calls=%async_computation.7 | async-start | bytes 8388608
  124.9 1.9 copy-start.9
  168.2 77.4 %all-to-all-start.1 = ((bf16[128,160,128]{2,1,0:T(8,128)(2,1)}), bf16[128,160,128]{2,1,0:T(8,128)(2,1)}, u32[]{:S(2)}, u32[]{:S(2)}) async-start(bf16[128,160,128]{2,1,0:T(8,128)(2,1)} %reshape_reshape.13), calls=%async_computation.1 | async-start | bytes 10485760 | tf_op jit(solution)/shard_map/all_to_all | solution.py:200
  180.7 19.2 %slice-start = ((s8[5242880]{0:T(1024)(128)(4,1)}), s8[1048576]{0:T(1024)(128)(4,1)S(1)}, s32[]{:S(2)}) async-start(s8[5242880]{0:T(1024)(128)(4,1)} %bitcast.29), calls=%async_computation.4 | async-start | bytes 2097152
  189.6 10.3 %slice-start.1 = ((s8[5242880]{0:T(1024)(128)(4,1)}), s8[4194304]{0:T(1024)(128)(4,1)S(1)}, s32[]{:S(2)}) async-start(s8[5242880]{0:T(1024)(128)(4,1)} %bitcast.29), calls=%async_computation.5 | async-start | bytes 8388608
  200.0 17.5 %copy-start.6 = (f32[4096]{0:T(1024)S(1)}, f32[4096]{0:T(1024)}, u32[]{:S(2)}) copy-start(f32[4096]{0:T(1024)} %param.8) | copy-start | bytes 49156
  232.1 26.0 %copy-start.2 = (bf16[128,4096]{1,0:T(8,128)(2,1)S(1)}, bf16[128,4096]{1,0:T(8,128)(2,1)}, u32[]{:S(2)}) copy-start(bf16[128,4096]{1,0:T(8,128)(2,1)} %layer_in.5) | copy-start | bytes 3145732
  245.6 80.9 %all-to-all-start.3 = ((bf16[128,168,128]{2,1,0:T(8,128)(2,1)}), bf16[128,168,128]{2,1,0:T(8,128)(2,1)}, u32[]{:S(2)}, u32[]{:S(2)}) async-start(bf16[128,168,128]{2,1,0:T(8,128)(2,1)} %fusion.11), calls=%async_computation.3 | async-start | bytes 11010048 | tf_op jit(solution)/shard_map/all_to_all | solution.py:200

commit v2 on v1

--- a/solution.py
+++ b/solution.py
@@ -1,3 +1,5 @@
+import functools
+
 import jax
 import jax.numpy as jnp
 from jax import lax
@@ -14,7 +16,9 @@
 BF16 = jnp.bfloat16
 VMEM = pl.BlockSpec(memory_space=pltpu.VMEM)
 SMEM = pl.BlockSpec(memory_space=pltpu.SMEM)
+HBM = pl.BlockSpec(memory_space=pltpu.HBM)
 PARAMS = pltpu.CompilerParams(vmem_limit_bytes=40 * 1024 * 1024)
+WHOLE = pltpu.CompilerParams(vmem_limit_bytes=60 * 1024 * 1024)
 
 
 def zero_fill(ref):
@@ -41,46 +45,96 @@
     return pl.ds(pl.multiple_of(slot * pieces, pieces), pieces)
 
 
-def send_rows_kernel(routes, layer_in, gain, out, place, rows, count):
+def send_rows_kernel(
+    chip_count, routes_in, layer_in, gain, out, place_out, inverse_out,
+    routes, x, gain_row, spread, packed, staged, inverses, place, count, table, in_sems, out_sems,
+):
     tokens, width = layer_in.shape
     pieces = width // LANES
     top = routes.shape[0]
-
-    def clear(i, carry):
-        count[i] = 0
-        return carry
-
-    lax.fori_loop(0, count.shape[0], clear, 0)
-    zero_fill(out)
-
-    def normalise(group, carry):
-        first = pl.multiple_of(group * GROUP, GROUP)
-        square = jnp.zeros((GROUP, LANES), F32)
-        for piece in range(pieces):
-            x = columns_of(layer_in, first, piece)
-            square = square + x * x
-        root_mean = jnp.sqrt(jnp.sum(square, axis=-1, keepdims=True) / width + EPSILON)
-        inverse = 1.0 / root_mean
-        for piece in range(pieces):
-            unit = columns_of(layer_in, first, piece) * inverse
-            rows[strip(group, piece, pieces), :] = (
-                unit * gain[:, piece * LANES : (piece + 1) * LANES]
-            )
-        return carry
-
-    lax.fori_loop(0, tokens // GROUP, normalise, 0)
-
-    def place_token(token, carry):
-        row = rows[token_rows(token, pieces), :].astype(BF16)
-        for k in range(top):
-            expert = routes[k, token]
-            slot = count[expert]
-            count[expert] = slot + 1
-            place[k, token] = expert * 8 + slot
-            out[expert, slot_rows(slot, pieces), :] = row
-        return carry
-
-    lax.fori_loop(0, tokens, place_token, 0)
+    peers = out.shape[0]
+    slots = out.shape[1] // pieces
+    cores = peers // chip_count
+    in_parts, out_parts = in_sems.shape[0] - 2, out_sems.shape[0] - 2
+    part = tokens // in_parts
+    copies = []
+    for i in range(in_parts):
+        cut = pl.ds(i * part, part)
+        copies.append(pltpu.make_async_copy(layer_in.at[cut], x.at[cut], in_sems.at[i]))
+    gain_copy = pltpu.make_async_copy(gain, gain_row, in_sems.at[in_parts])
+    routes_copy = pltpu.make_async_copy(routes_in, routes, in_sems.at[in_parts + 1])
+    copies[0].start()
+    gain_copy.start()
+    routes_copy.start()
+    for copy in copies[1:]:
+        copy.start()
+
+    def clear(chip, carry):
+        for core in range(cores):
+            first = (chip * cores + core) * 8
+            count[core * chip_count + chip] = first
+            for slot in range(slots):
+                table[first + slot] = tokens
+        return carry
+
+    lax.fori_loop(0, chip_count, clear, 0)
+    packed[pl.ds(tokens * pieces, pieces), :] = jnp.zeros((pieces, LANES), BF16)
+    routes_copy.wait()
+    gain_copy.wait()
+
+    def take_part(first):
+        groups = range(first, first + part, GROUP)
+        for at in groups:
+            square = jnp.zeros((GROUP, LANES), F32)
+            for piece in range(pieces):
+                values = columns_of(x, at, piece)
+                square = square + values * values
+            root_mean = jnp.sqrt(jnp.sum(square, axis=-1, keepdims=True) / width + EPSILON)
+            inverses[pl.ds(at, GROUP), :] = jnp.broadcast_to(1.0 / root_mean, (GROUP, LANES))
+        for at in groups:
+            inverse = inverses[pl.ds(at, GROUP), :]
+            for piece in range(pieces):
+                unit = columns_of(x, at, piece) * inverse
+                spread[pl.ds((at - first) * pieces + piece, GROUP, stride=pieces), :] = (
+                    unit * gain_row[:, piece * LANES : (piece + 1) * LANES]
+                )
+        packed[first * pieces : (first + part) * pieces, :] = spread[...].astype(BF16)
+        for token in range(first, first + part):
+            experts = [routes[k, token] for k in range(top)]
+            wheres = [count[expert] for expert in experts]
+            for k in range(top):
+                count[experts[k]] = wheres[k] + 1
+                place[k, token] = wheres[k]
+                table[wheres[k]] = token
+
+    for i in range(in_parts):
+        copies[i].wait()
+        take_part(i * part)
+    sent = [
+        pltpu.make_async_copy(place, place_out, out_sems.at[out_parts]),
+        pltpu.make_async_copy(inverses, inverse_out, out_sems.at[out_parts + 1]),
+    ]
+    for copy in sent:
+        copy.start()
+    step = peers // out_parts
+
+    def fill(pair, carry):
+        for i in range(2):
+            peer = pair * 2 + i
+            chosen = [table[peer * 8 + slot] for slot in range(slots)]
+            for slot in range(slots):
+                staged[peer, slot * pieces : (slot + 1) * pieces, :] = packed[
+                    token_rows(chosen[slot], pieces), :
+                ]
+        return carry
+
+    for i in range(out_parts):
+        lax.fori_loop(i * step // 2, (i + 1) * step // 2, fill, 0)
+        cut = pl.ds(i * step, step)
+        sent.append(pltpu.make_async_copy(staged.at[cut], out.at[cut], out_sems.at[i]))
+        sent[-1].start()
+    for copy in sent:
+        copy.wait()
 
 
 def send_grads_kernel(place, weights, out_grad, out, rows):
@@ -101,7 +155,7 @@
         row = rows[token_rows(token, pieces), :]
         for k in range(top):
             where = place[k, token]
-            out[where // 8, slot_rows(where % 8, pieces), :] = (row * weights[k, token]).astype(BF16)
+            out[where >> 3, slot_rows(where & 7, pieces), :] = (row * weights[k, token]).astype(BF16)
         return carry
 
     lax.fori_loop(0, tokens, place_token, 0)
@@ -125,7 +179,7 @@
         total = jnp.zeros((pieces, LANES), F32)
         for k in range(top):
             where = place[k, token]
-            row = returned[where // 8, slot_rows(where % 8, pieces), :].astype(F32)
+            row = returned[where >> 3, slot_rows(where & 7, pieces), :].astype(F32)
             total = total + weights[k, token] * row
             dots[k, pl.ds(token, 1), :] = jnp.sum(row * grad, axis=0, keepdims=True)
         sums[token_rows(token, pieces), :] = total
@@ -147,49 +201,96 @@
     lax.fori_loop(0, tokens // GROUP, finish, 0)
 
 
-def input_grad_kernel(place, layer_in, gain, out_grad, returned, input_grad, gain_grad, sums):
+def input_grad_kernel(
+    place_in, layer_in, inverse_in, gain_in, out_grad, returned, input_grad, gain_grad,
+    place, x, inverse, gain_rows, grad, held, units, sums, dots, result, in_sems, sems, out_sems,
+):
     tokens, width = out_grad.shape
     pieces = width // LANES
     top = place.shape[0]
     peers = returned.shape[0]
+    share = gain_grad.shape[1]
     body_rows = returned.shape[1] - EXTRA
-
-    def combine(token, carry):
-        total = jnp.zeros((pieces, LANES), F32)
-        for k in range(top):
-            where = place[k, token]
-            total = total + returned[where // 8, slot_rows(where % 8, pieces), :].astype(F32)
-        sums[token_rows(token, pieces), :] = total
-        return carry
-
-    lax.fori_loop(0, tokens, combine, 0)
+    parts = sems.shape[0]
+    step = peers // parts
+    small = [
+        pltpu.make_async_copy(source, target, in_sems.at[i])
+        for i, (source, target) in enumerate(
+            ((layer_in, x), (inverse_in, inverse), (place_in, place), (gain_in, gain_rows), (out_grad, grad))
+        )
+    ]
+    for copy in small[:2]:
+        copy.start()
+    copies = []
+    for i in range(parts):
+        cut = pl.ds(i * step, step)
+        copies.append(pltpu.make_async_copy(returned.at[cut], held.at[cut], sems.at[i]))
+        copies[i].start()
+    for copy in small[2:]:
+        copy.start()
+    for copy in small[:2]:
+        copy.wait()
+
+    def spread(group, carry):
+        first = pl.multiple_of(group * GROUP, GROUP)
+        scale = inverse[pl.ds(first, GROUP), :]
+        for piece in range(pieces):
+            units[strip(group, piece, pieces), :] = columns_of(x, first, piece) * scale
+        return carry
+
+    lax.fori_loop(0, tokens // GROUP, spread, 0)
+    for copy in small[2:] + copies:
+        copy.wait()
+
+    def combine(block, carry):
+        for i in range(4):
+            token = block * 4 + i
+            wheres = [place[k, token] for k in range(top)]
+            total = jnp.zeros((pieces, LANES), F32)
+            for where in wheres:
+                total = total + held[where >> 3, slot_rows(where & 7, pieces), :].astype(F32)
+            q = total * gain_rows[...]
+            sums[token_rows(token, pieces), :] = q
+            along = q * units[token_rows(token, pieces), :]
+            dots[pl.ds(token, 1), :] = jnp.sum(along, axis=0, keepdims=True)
+        return carry
+
+    lax.fori_loop(0, tokens // 4, combine, 0)
+    means = jnp.sum(dots[...], axis=-1, keepdims=True) / width
+    dots[...] = inverse[...] * means
 
     def finish(group, carry):
         first = pl.multiple_of(group * GROUP, GROUP)
-        square = jnp.zeros((GROUP, LANES), F32)
-        along = jnp.zeros((GROUP, LANES), F32)
-        for piece in range(pieces):
-            x = columns_of(layer_in, first, piece)
-            q = sums[strip(group, piece, pieces), :] * gain[:, piece * LANES : (piece + 1) * LANES]
-            square = square + x * x
-            along = along + q * x
-        inverse = 1.0 / jnp.sqrt(jnp.sum(square, axis=-1, keepdims=True) / width + EPSILON)
-        mean = jnp.sum(along, axis=-1, keepdims=True) * inverse / width
+        scale = inverse[pl.ds(first, GROUP), :]
+        lean = dots[pl.ds(first, GROUP), :]
         for piece in range(pieces):
             cut = slice(piece * LANES, (piece + 1) * LANES)
-            unit = columns_of(layer_in, first, piece) * inverse
-            q = sums[strip(group, piece, pieces), :] * gain[:, cut]
-            input_grad[pl.ds(first, GROUP), cut] = (
-                columns_of(out_grad, first, piece) + (q - unit * mean) * inverse
+            q = sums[strip(group, piece, pieces), :]
+            result[pl.ds(first, GROUP), cut] = (
+                columns_of(grad, first, piece) + (q - columns_of(x, first, piece) * lean) * scale
             ).astype(BF16)
         return carry
 
-    lax.fori_loop(0, tokens // GROUP, finish, 0)
-
-    def add_peer(peer, total):
-        return total + returned[peer, body_rows : body_rows + EXTRA, :].astype(F32)
-
-    gain_grad[...] = lax.fori_loop(0, peers, add_peer, jnp.zeros((EXTRA, LANES), F32))
+    out_parts = out_sems.shape[0]
+    part = tokens // out_parts
+    sent = []
+    for i in range(out_parts):
+        lax.fori_loop(i * part // GROUP, (i + 1) * part // GROUP, finish, 0)
+        cut = pl.ds(i * part, part)
+        sent.append(pltpu.make_async_copy(result.at[cut], input_grad.at[cut], out_sems.at[i]))
+        sent[i].start()
+
+    def add_peers(block, total):
+        for i in range(8):
+            total = total + held[block * 8 + i, body_rows : body_rows + EXTRA, :].astype(F32)
+        return total
+
+    total = lax.fori_loop(0, peers // 8, add_peers, jnp.zeros((EXTRA, LANES), F32))[0:1]
+    gain_grad[...] = (
+        total[:, :share] + total[:, share : 2 * share] + total[:, 2 * share : 3 * share]
+    )
+    for copy in sent:
+        copy.wait()
 
 
 def transposed(left, right):
@@ -197,7 +298,7 @@
 
 
 def exchange(buffer):
-    return lax.all_to_all(buffer, AXES, split_axis=0, concat_axis=0, tiled=True)
+    return lax.all_to_all(buffer, ("dev", "role"), split_axis=0, concat_axis=0, tiled=True)
 
 
 def three_parts(values):
@@ -213,6 +314,7 @@
     peers = lax.axis_size(AXES)
     slots = tokens * top * 5 // (4 * peers)
     pieces = width // LANES
+    chips = lax.axis_size("dev")
     hidden_units = expert_down.shape[1]
     row_count = peers * slots
     block = (peers, slots * pieces, LANES)
@@ -221,16 +323,31 @@
     weights = gate_weights.T
     token_scratch = pltpu.VMEM((tokens * pieces, LANES), F32)
 
-    send_rows, place = pl.pallas_call(
-        send_rows_kernel,
+    in_parts, out_parts = 4, 8
+    send_rows, place, inverse = pl.pallas_call(
+        functools.partial(send_rows_kernel, chips),
         out_shape=(
             jax.ShapeDtypeStruct(block, BF16),
             jax.ShapeDtypeStruct((top, tokens), jnp.int32),
+            jax.ShapeDtypeStruct((tokens, LANES), F32),
         ),
-        in_specs=[SMEM, VMEM, VMEM],
-        out_specs=(VMEM, SMEM),
-        scratch_shapes=[token_scratch, pltpu.SMEM((peers,), jnp.int32)],
-        compiler_params=PARAMS,
+        in_specs=[HBM, HBM, HBM],
+        out_specs=(HBM, HBM, HBM),
+        scratch_shapes=[
+            pltpu.SMEM((top, tokens), jnp.int32),
+            pltpu.VMEM((tokens, width), BF16),
+            pltpu.VMEM((1, width), F32),
+            pltpu.VMEM((tokens // in_parts * pieces, LANES), F32),
+            pltpu.VMEM(((tokens + 1) * pieces, LANES), BF16),
+            pltpu.VMEM(block, BF16),
+            pltpu.VMEM((tokens, LANES), F32),
+            pltpu.SMEM((top, tokens), jnp.int32),
+            pltpu.SMEM((peers,), jnp.int32),
+            pltpu.SMEM((peers * 8,), jnp.int32),
+            pltpu.SemaphoreType.DMA((in_parts + 2,)),
+            pltpu.SemaphoreType.DMA((out_parts + 2,)),
+        ],
+        compiler_params=WHOLE,
         name="send_rows",
     )(by_choice, layer_in, gain)
     arrived = exchange(send_rows).reshape(row_count, pieces, LANES).reshape(row_count, width)
@@ -263,7 +380,13 @@
     back_rows = transposed(pre_grad, w_gate_up).astype(BF16)
     terms = jnp.sum(back_rows.astype(F32) * arrived.astype(F32), axis=0) / norm_gain
     share = width // peers
-    parts = jnp.concatenate([p.reshape(peers, share) for p in three_parts(terms)], axis=-1)
+    parts = jnp.concatenate(
+        [
+            jnp.swapaxes(p.reshape(peers // chips, chips, share), 0, 1).reshape(peers, share)
+            for p in three_parts(terms)
+        ],
+        axis=-1,
+    )
     parts = jnp.pad(parts[:, None, :], ((0, 0), (0, EXTRA - 1), (0, LANES - 3 * share)))
     send_back = jnp.concatenate(
         [back_rows.reshape(row_count, pieces, LANES).reshape(block), parts], axis=1
@@ -283,19 +406,33 @@
         name="outputs",
     )(place, weights, layer_in, out_grad, returned)
 
-    input_grad, gain_sums = pl.pallas_call(
+    input_grad, gain_grad = pl.pallas_call(
         input_grad_kernel,
         out_shape=(
             jax.ShapeDtypeStruct((tokens, width), BF16),
-            jax.ShapeDtypeStruct((EXTRA, LANES), F32),
+            jax.ShapeDtypeStruct((1, share), F32),
         ),
-        in_specs=[SMEM, VMEM, VMEM, VMEM, VMEM],
-        out_specs=(VMEM, VMEM),
-        scratch_shapes=[token_scratch],
-        compiler_params=PARAMS,
+        in_specs=[HBM] * 6,
+        out_specs=(HBM, VMEM),
+        scratch_shapes=[
+            pltpu.SMEM((top, tokens), jnp.int32),
+            pltpu.VMEM((tokens, width), BF16),
+            pltpu.VMEM((tokens, LANES), F32),
+            pltpu.VMEM((pieces, LANES), F32),
+            pltpu.VMEM((tokens, width), BF16),
+            pltpu.VMEM(came_back.shape, BF16),
+            token_scratch,
+            token_scratch,
+            pltpu.VMEM((tokens, LANES), F32),
+            pltpu.VMEM((tokens, width), BF16),
+            pltpu.SemaphoreType.DMA((5,)),
+            pltpu.SemaphoreType.DMA((8,)),
+            pltpu.SemaphoreType.DMA((4,)),
+        ],
+        compiler_params=WHOLE,
         name="input_grad",
-    )(place, layer_in, gain, out_grad, came_back)
-    gain_grad = jnp.sum(gain_sums[0, : 3 * share].reshape(3, share), axis=0)
+    )(place, layer_in, inverse, norm_gain.reshape(pieces, LANES), out_grad, came_back)
+    gain_grad = gain_grad.reshape(share)
     return (layer_out, input_grad, gate_grad.T, gain_grad)
 
 

time: 345 us -> 304 us (0.88); the launches traced: 339 us -> 302 us
  starting transfers between devices: 49.3 us -> 28.8 us
  Pallas kernels: 40.4 us -> 30.2 us
  local copies, waits for them, and re-layouts: 45.4 us -> 40.4 us
    all_to_all x4, starting transfers between devices: 49.3 us -> 28.8 us  [exchange(): lax.all_to_all(buffer, ('dev', 'role'), split_axis=0, concat_axis=0, tile...]
    unnamed x28 -> x22, local copies, waits for them, and re-layouts: 9.26 us -> 4.29 us
    pallas_call x1, Pallas kernels: 12 us -> 8.5 us  [body(): pl.pallas_call(input_grad_kernel, out_shape=(jax.ShapeDtypeStruct((tokens...]
  transfers between devices with their start and end apart: 4 -> 4, of which waited for: 4 -> 4; matrix products, arithmetic and copies ran while one was open for 26% -> 29% of each run, Pallas kernels for 6% -> 5%
where the time goes in v2:
time: 304 us; the launch traced here: 302 us
  waiting for transfers between devices  150 us (49%)
  matrix products  46.4 us (15%)
  local copies, waits for them, and re-layouts  40.4 us (13%)
  Pallas kernels  30.2 us (10%)
  starting transfers between devices  28.8 us (9%)
  other arithmetic  5.45 us (2%)
    all_to_all x4, waiting for transfers between devices, exchange(): lax.all_to_all(buffer, ('dev', 'role'), split_axis=0, concat_axis=0, tile...  150 us
    all_to_all x4, starting transfers between devices, exchange(): lax.all_to_all(buffer, ('dev', 'role'), split_axis=0, concat_axis=0, tile...  28.8 us
    dot_general x2, matrix products, transposed(): lax.dot_general(left, right, (((1,), (1,)), ((), ())), preferred_element_...  27.7 us
    dot_general x1, matrix products, body(): projected = jnp.dot(arrived, w_gate_up, preferred_element_type=F32)  12.5 us
    pallas_call x1, Pallas kernels, body(): pl.pallas_call(outputs_kernel, out_shape=(jax.ShapeDtypeStruct((tokens, w...  10.1 us
    another operation x1, local copies, waits for them, and re-layouts, body(): exchange(send_rows).reshape(row_count, pieces, LANES)  8.97 us
    another operation x1, local copies, waits for them, and re-layouts, body(): back_rows.reshape(row_count, pieces, LANES).reshape(block)  8.94 us
    another operation x1, local copies, waits for them, and re-layouts, body(): expert_rows.reshape(row_count, pieces, LANES).reshape(block)  8.91 us
  transfers between devices with their start and end apart: 4, of which 4 were waited for; matrix products, arithmetic and copies ran while one was open for 29% of the time, Pallas kernels for 5%

profile of v2, /device:TPU:1, one launch (start us, length us, event | category | flops | bytes accessed | tf_op | source)
XLA Modules:
  0.0 302.4 jit_solution(9250732786729220678)
XLA Ops:
  0.6 6.0 %send_rows.1 = (bf16[128,160,128]{2,1,0:T(8,128)(2,1)}, s32[4,128]{1,0:T(4,128)}, f32[128,128]{1,0:T(8,128)}) custom-call(s32[4,128]{1,0:T(4,128)} %bitcast.44, bf16[128,4096]{1,0:T(8,128)(2,1)} %layer_in.5, f32[1,4096]{1,0:T(1,128)} %bitcast.36), custom_call_target="tpu_custom_call" | custom-call | tf_op jit(solution)/shard_map/send_rows/pallas_call | solution.py:327
  6.7 0.0 copy-start.2
  6.7 0.0 copy-start.3
  6.7 0.0 copy-start.4
  6.7 11.9 %all-to-all-start = ((bf16[128,160,128]{2,1,0:T(8,128)(2,1)}), bf16[128,160,128]{2,1,0:T(8,128)(2,1)}, u32[]{:S(2)}, u32[]{:S(2)}) async-start(bf16[128,160,128]{2,1,0:T(8,128)(2,1)} %get-tuple-element.12), calls=%async_computation | async-start | bytes 10485760 | tf_op jit(solution)/shard_map/all_to_all | solution.py:301
  18.6 0.0 copy-done.2
  18.6 0.0 copy-done.3
  18.6 0.0 copy-done.4
  18.6 5.5 %send_grads.1 = bf16[128,160,128]{2,1,0:T(8,128)(2,1)S(1)} custom-call(s32[4,128]{1,0:T(4,128)S(1)} %copy-done.3, f32[4,128]{1,0:T(4,128)S(1)} %bitcast.32, bf16[128,4096]{1,0:T(8,128)(2,1)S(1)} %copy-done.2), custom_call_target="tpu_custom_call" | custom-call | tf_op jit(solution)/shard_map/send_grads/pallas_call | solution.py:355
  24.1 0.0 copy-start
  24.1 2.4 copy-done
  26.5 55.9 %all-to-all-done = bf16[128,160,128]{2,1,0:T(8,128)(2,1)} async-done(((bf16[128,160,128]{2,1,0:T(8,128)(2,1)}), bf16[128,160,128]{2,1,0:T(8,128)(2,1)}, u32[]{:S(2)}, u32[]{:S(2)}) %all-to-all-start) | async-done | bytes 5242912 | tf_op jit(solution)/shard_map/all_to_all | solution.py:301
  82.4 5.6 %all-to-all-start.2 = ((bf16[128,160,128]{2,1,0:T(8,128)(2,1)}), bf16[128,160,128]{2,1,0:T(8,128)(2,1)}, u32[]{:S(2)}, u32[]{:S(2)}) async-start(bf16[128,160,128]{2,1,0:T(8,128)(2,1)} %copy-done), calls=%async_computation.2 | async-start | bytes 10485760 | tf_op jit(solution)/shard_map/all_to_all | solution.py:301
  88.0 0.0 slice-start.2
  88.0 9.0 %reshape_reshape.12 = bf16[640,4096]{1,0:T(8,128)(2,1)} reshape(bf16[128,160,128]{2,1,0:T(8,128)(2,1)} %all-to-all-done) | data formatting | bytes 10485760 | tf_op jit(solution)/shard_map/reshape;reshape | solution.py:353
  97.0 0.0 slice-start.3
  97.0 12.5 %fusion.2 = f32[640,1536]{1,0:T(8,128)S(1)} fusion(bf16[640,4096]{1,0:T(8,128)(2,1)} %reshape_reshape.12, bf16[1,4096,1536]{2,1,0:T(8,128)(2,1)} %param.12), kind=kOutput, calls=%fused_computation.2 | convolution fusion | flops 8053063680 | bytes 21757952 | tf_op jit(solution)/shard_map/dot_general | solution.py:368
  109.5 0.0 copy-start.6
  109.6 1.9 copy-done.6
  111.4 0.0 slice-done.2
  111.4 0.0 slice-done.3
  111.4 6.1 %convolution_convert_fusion = bf16[640,4096]{1,0:T(8,128)(2,1)} fusion(bf16[1,768,4096]{2,1,0:T(8,128)(2,1)S(1)} %bitcast.46, f32[640,1536]{1,0:T(8,128)S(1)} %fusion.2), kind=kOutput, calls=%fused_computation.8 | convolution fusion | flops 4032102400 | bytes 15466496 | tf_op jit(solution)/shard_map/dot_general | solution.py:374
  117.6 8.9 %reshape_reshape.13 = bf16[128,160,128]{2,1,0:T(8,128)(2,1)} reshape(bf16[640,4096]{1,0:T(8,128)(2,1)} %convolution_convert_fusion) | data formatting | bytes 10485760 | tf_op jit(solution)/shard_map/reshape;reshape | solution.py:375
  126.5 25.4 %all-to-all-done.2 = bf16[128,160,128]{2,1,0:T(8,128)(2,1)} async-done(((bf16[128,160,128]{2,1,0:T(8,128)(2,1)}), bf16[128,160,128]{2,1,0:T(8,128)(2,1)}, u32[]{:S(2)}, u32[]{:S(2)}) %all-to-all-start.2) | async-done | bytes 5242912 | tf_op jit(solution)/shard_map/all_to_all | solution.py:301
  151.9 5.6 %all-to-all-start.1 = ((bf16[128,160,128]{2,1,0:T(8,128)(2,1)}), bf16[128,160,128]{2,1,0:T(8,128)(2,1)}, u32[]{:S(2)}, u32[]{:S(2)}) async-start(bf16[128,160,128]{2,1,0:T(8,128)(2,1)} %reshape_reshape.13), calls=%async_computation.1 | async-start | bytes 10485760 | tf_op jit(solution)/shard_map/all_to_all | solution.py:301
  157.5 0.0 slice-start
  157.6 8.9 %reshape_reshape.14 = bf16[640,4096]{1,0:T(8,128)(2,1)} reshape(bf16[128,160,128]{2,1,0:T(8,128)(2,1)} %all-to-all-done.2) | data formatting | bytes 10485760 | tf_op jit(solution)/shard_map/reshape;reshape | solution.py:364
  166.4 0.0 slice-start.1
  166.4 10.3 %multiply_convert_fusion.1 = (bf16[640,768]{1,0:T(8,128)(2,1)S(1)}, bf16[640,768]{1,0:T(8,128)(2,1)S(1)}) fusion(f32[640,1536]{1,0:T(8,128)} %copy-done.6, bf16[640,4096]{1,0:T(8,128)(2,1)} %reshape_reshape.14, bf16[1,768,4096]{2,1,0:T(8,128)(2,1)} %param.13), kind=kOutput, calls=%fused_computation.17 | convolution fusion | flops 4032921600 | bytes 17432576 | tf_op jit(solution)/shard_map/dot_general | solution.py:297
  176.7 0.0 slice-done
  176.8 0.0 slice-done.1
  176.8 0.0 copy-start.5
  176.8 17.5 %multiply_reduce_fusion = (f32[4096]{0:T(1024)S(1)}, bf16[640,4096]{1,0:T(8,128)(2,1)}) fusion(bf16[640,4096]{1,0:T(8,128)(2,1)S(1)} %bitcast.35, bf16[1,4096,1536]{2,1,0:T(8,128)(2,1)} %param.12, bf16[640,768]{1,0:T(8,128)(2,1)S(1)} %get-tuple-element.19, bf16[640,768]{1,0:T(8,128)(2,1)S(1)} %get-tuple-element.18), kind=kOutput, calls=%fused_computation.6 | convolution fusion | flops 8070098944 | bytes 25051136 | tf_op jit(solution)/shard_map/dot_general | solution.py:297
  194.2 0.0 copy-done.5
  194.3 0.1 reshape.41
  194.4 0.1 reshape.37
  194.5 0.1 reshape.39
  194.6 0.1 maximum_bitcast_fusion
  194.7 0.1 copy.16
  194.8 8.9 %reshape_reshape.15 = bf16[128,160,128]{2,1,0:T(8,128)(2,1)} reshape(bf16[640,4096]{1,0:T(8,128)(2,1)} %get-tuple-element.24) | data formatting | bytes 10485760 | tf_op jit(solution)/shard_map/reshape;reshape | solution.py:392
  203.7 5.3 %fusion.11 = bf16[128,168,128]{2,1,0:T(8,128)(2,1)} fusion(bf16[128,1,96]{2,1,0:T(2,128)(2,1)S(1)} %copy.16, bf16[128,160,128]{2,1,0:T(8,128)(2,1)} %reshape_reshape.15), kind=kLoop, calls=%fused_computation.12 | loop fusion | flops 16515072 | bytes 10772480 | tf_op jit(solution)/shard_map/concatenate | solution.py:391
  209.1 0.0 copy-start.1
  209.1 12.3 %all-to-all-done.1.returned = bf16[128,160,128]{2,1,0:T(8,128)(2,1)} async-done(((bf16[128,160,128]{2,1,0:T(8,128)(2,1)}), bf16[128,160,128]{2,1,0:T(8,128)(2,1)}, u32[]{:S(2)}, u32[]{:S(2)}) %all-to-all-start.1) | async-done | bytes 5242912 | tf_op jit(solution)/shard_map/all_to_all | solution.py:301
  221.4 5.6 %all-to-all-start.3 = ((bf16[128,168,128]{2,1,0:T(8,128)(2,1)}), bf16[128,168,128]{2,1,0:T(8,128)(2,1)}, u32[]{:S(2)}, u32[]{:S(2)}) async-start(bf16[128,168,128]{2,1,0:T(8,128)(2,1)} %fusion.11), calls=%async_computation.3 | async-start | bytes 11010048 | tf_op jit(solution)/shard_map/all_to_all | solution.py:301
  227.1 0.0 copy-done.1
  227.1 10.1 %outputs.1 = (bf16[128,4096]{1,0:T(8,128)(2,1)}, f32[4,128]{1,0:T(4,128)}) custom-call(s32[4,128]{1,0:T(4,128)S(1)} %copy-done.3, f32[4,128]{1,0:T(4,128)S(1)} %bitcast.33, bf16[128,4096]{1,0:T(8,128)(2,1)S(1)} %copy-done.1, bf16[128,4096]{1,0:T(8,128)(2,1)S(1)} %copy-done.2, bf16[128,160,128]{2,1,0:T(8,128)(2,1)} %all-to-all-done.1.returned), custom_call_target="tpu_custom_call" | custom-call | tf_op jit(solution)/shard_map/outputs/pallas_call | solution.py:396
  237.2 56.5 %all-to-all-done.3.returned = bf16[128,168,128]{2,1,0:T(8,128)(2,1)} async-done(((bf16[128,168,128]{2,1,0:T(8,128)(2,1)}), bf16[128,168,128]{2,1,0:T(8,128)(2,1)}, u32[]{:S(2)}, u32[]{:S(2)}) %all-to-all-start.3) | async-done | bytes 5505056 | tf_op jit(solution)/shard_map/all_to_all | solution.py:301
  293.7 8.5 %input_grad.1 = (bf16[128,4096]{1,0:T(8,128)(2,1)}, f32[1,32]{1,0:T(1,128)}) custom-call(s32[4,128]{1,0:T(4,128)} %get-tuple-element.11.place.place_in, bf16[128,4096]{1,0:T(8,128)(2,1)} %layer_in.5, f32[128,128]{1,0:T(8,128)} %get-tuple-element.14.inverse_in, f32[32,128]{1,0:T(8,128)} %bitcast.37, bf16[128,4096]{1,0:T(8,128)(2,1)} %out_grad.5, ...), custom_call_target="tpu_custom_call" | custom-call | tf_op jit(solution)/shard_map/input_grad/pallas_call | solution.py:409
  (6 shorter events, 0.1 us)
Async XLA Ops:
  6.7 11.9 %copy-start.2 = (bf16[128,4096]{1,0:T(8,128)(2,1)S(1)}, bf16[128,4096]{1,0:T(8,128)(2,1)}, u32[]{:S(2)}) copy-start(bf16[128,4096]{1,0:T(8,128)(2,1)} %out_grad.5) | copy-start | bytes 3145732
  6.7 11.9 %copy-start.3 = (s32[4,128]{1,0:T(4,128)S(1)}, s32[4,128]{1,0:T(4,128)}, u32[]{:S(2)}) copy-start(s32[4,128]{1,0:T(4,128)} %get-tuple-element.11.place.place_in) | copy-start | bytes 6148
  6.7 11.9 %copy-start.4 = (f32[128,4]{0,1:T(4,128)S(1)}, f32[128,4]{0,1:T(4,128)}, u32[]{:S(2)}) copy-start(f32[128,4]{0,1:T(4,128)} %param.10) | copy-start | bytes 6148
  6.7 75.7 %all-to-all-start = ((bf16[128,160,128]{2,1,0:T(8,128)(2,1)}), bf16[128,160,128]{2,1,0:T(8,128)(2,1)}, u32[]{:S(2)}, u32[]{:S(2)}) async-start(bf16[128,160,128]{2,1,0:T(8,128)(2,1)} %get-tuple-element.12), calls=%async_computation | async-start | bytes 10485760 | tf_op jit(solution)/shard_map/all_to_all | solution.py:301
  24.1 2.4 copy-start
  82.4 69.5 %all-to-all-start.2 = ((bf16[128,160,128]{2,1,0:T(8,128)(2,1)}), bf16[128,160,128]{2,1,0:T(8,128)(2,1)}, u32[]{:S(2)}, u32[]{:S(2)}) async-start(bf16[128,160,128]{2,1,0:T(8,128)(2,1)} %copy-done), calls=%async_computation.2 | async-start | bytes 10485760 | tf_op jit(solution)/shard_map/all_to_all | solution.py:301
  88.0 23.4 %slice-start.2 = ((s8[6291456]{0:T(1024)(128)(4,1)}), s8[2097152]{0:T(1024)(128)(4,1)S(1)}, s32[]{:S(2)}) async-start(s8[6291456]{0:T(1024)(128)(4,1)} %bitcast.45), calls=%async_computation.6 | async-start | bytes 4194304
  97.0 14.4 %slice-start.3 = ((s8[6291456]{0:T(1024)(128)(4,1)}), s8[4194304]{0:T(1024)(128)(4,1)S(1)}, s32[]{:S(2)}) async-start(s8[6291456]{0:T(1024)(128)(4,1)} %bitcast.45), calls=%async_computation.7 | async-start | bytes 8388608
  109.5 1.9 copy-start.6
  151.9 69.5 %all-to-all-start.1 = ((bf16[128,160,128]{2,1,0:T(8,128)(2,1)}), bf16[128,160,128]{2,1,0:T(8,128)(2,1)}, u32[]{:S(2)}, u32[]{:S(2)}) async-start(bf16[128,160,128]{2,1,0:T(8,128)(2,1)} %reshape_reshape.13), calls=%async_computation.1 | async-start | bytes 10485760 | tf_op jit(solution)/shard_map/all_to_all | solution.py:301
  157.5 19.2 %slice-start = ((s8[5242880]{0:T(1024)(128)(4,1)}), s8[1048576]{0:T(1024)(128)(4,1)S(1)}, s32[]{:S(2)}) async-start(s8[5242880]{0:T(1024)(128)(4,1)} %bitcast.34), calls=%async_computation.4 | async-start | bytes 2097152
  166.4 10.3 %slice-start.1 = ((s8[5242880]{0:T(1024)(128)(4,1)}), s8[4194304]{0:T(1024)(128)(4,1)S(1)}, s32[]{:S(2)}) async-start(s8[5242880]{0:T(1024)(128)(4,1)} %bitcast.34), calls=%async_computation.5 | async-start | bytes 8388608
  176.8 17.5 %copy-start.5 = (f32[4096]{0:T(1024)S(1)}, f32[4096]{0:T(1024)}, u32[]{:S(2)}) copy-start(f32[4096]{0:T(1024)} %param.8) | copy-start | bytes 49156
  209.1 18.0 %copy-start.1 = (bf16[128,4096]{1,0:T(8,128)(2,1)S(1)}, bf16[128,4096]{1,0:T(8,128)(2,1)}, u32[]{:S(2)}) copy-start(bf16[128,4096]{1,0:T(8,128)(2,1)} %layer_in.5) | copy-start | bytes 3145732
  221.4 72.3 %all-to-all-start.3 = ((bf16[128,168,128]{2,1,0:T(8,128)(2,1)}), bf16[128,168,128]{2,1,0:T(8,128)(2,1)}, u32[]{:S(2)}, u32[]{:S(2)}) async-start(bf16[128,168,128]{2,1,0:T(8,128)(2,1)} %fusion.11), calls=%async_computation.3 | async-start | bytes 11010048 | tf_op jit(solution)/shard_map/all_to_all | solution.py:301

commit v3 on v2

--- a/solution.py
+++ b/solution.py
@@ -18,15 +18,17 @@
 SMEM = pl.BlockSpec(memory_space=pltpu.SMEM)
 HBM = pl.BlockSpec(memory_space=pltpu.HBM)
 PARAMS = pltpu.CompilerParams(vmem_limit_bytes=40 * 1024 * 1024)
+SMALL = pltpu.CompilerParams(vmem_limit_bytes=24 * 1024 * 1024)
 WHOLE = pltpu.CompilerParams(vmem_limit_bytes=60 * 1024 * 1024)
 
 
-def zero_fill(ref):
+def zero_fill(ref, step):
     def one(i, carry):
-        ref[i] = jnp.zeros(ref.shape[1:], ref.dtype)
-        return carry
-
-    lax.fori_loop(0, ref.shape[0], one, 0)
+        rows = pl.ds(pl.multiple_of(i * step, step), step)
+        ref[rows, :] = jnp.zeros((step, ref.shape[1]), ref.dtype)
+        return carry
+
+    lax.fori_loop(0, ref.shape[0] // step, one, 0)
 
 
 def columns_of(ref, first, piece):
@@ -41,8 +43,8 @@
     return pl.ds(pl.multiple_of(token * pieces, pieces), pieces)
 
 
-def slot_rows(slot, pieces):
-    return pl.ds(pl.multiple_of(slot * pieces, pieces), pieces)
+def slot_rows(where, pieces):
+    return pl.ds(pl.multiple_of(where, pieces), pieces)
 
 
 def send_rows_kernel(
@@ -55,6 +57,7 @@
     peers = out.shape[0]
     slots = out.shape[1] // pieces
     cores = peers // chip_count
+    shift = pieces.bit_length() - 1
     in_parts, out_parts = in_sems.shape[0] - 2, out_sems.shape[0] - 2
     part = tokens // in_parts
     copies = []
@@ -71,10 +74,10 @@
 
     def clear(chip, carry):
         for core in range(cores):
-            first = (chip * cores + core) * 8
-            count[core * chip_count + chip] = first
+            peer = chip * cores + core
+            count[core * chip_count + chip] = peer * (slots * pieces)
             for slot in range(slots):
-                table[first + slot] = tokens
+                table[peer * slots + slot] = tokens
         return carry
 
     lax.fori_loop(0, chip_count, clear, 0)
@@ -103,9 +106,9 @@
             experts = [routes[k, token] for k in range(top)]
             wheres = [count[expert] for expert in experts]
             for k in range(top):
-                count[experts[k]] = wheres[k] + 1
+                count[experts[k]] = wheres[k] + pieces
                 place[k, token] = wheres[k]
-                table[wheres[k]] = token
+                table[wheres[k] >> shift] = token
 
     for i in range(in_parts):
         copies[i].wait()
@@ -121,7 +124,7 @@
     def fill(pair, carry):
         for i in range(2):
             peer = pair * 2 + i
-            chosen = [table[peer * 8 + slot] for slot in range(slots)]
+            chosen = [table[peer * slots + slot] for slot in range(slots)]
             for slot in range(slots):
                 staged[peer, slot * pieces : (slot + 1) * pieces, :] = packed[
                     token_rows(chosen[slot], pieces), :
@@ -141,7 +144,7 @@
     tokens, width = out_grad.shape
     pieces = width // LANES
     top = place.shape[0]
-    zero_fill(out)
+    zero_fill(out, pieces * top)
 
     def spread(group, carry):
         first = pl.multiple_of(group * GROUP, GROUP)
@@ -154,8 +157,7 @@
     def place_token(token, carry):
         row = rows[token_rows(token, pieces), :]
         for k in range(top):
-            where = place[k, token]
-            out[where >> 3, slot_rows(where & 7, pieces), :] = (row * weights[k, token]).astype(BF16)
+            out[slot_rows(place[k, token], pieces), :] = (row * weights[k, token]).astype(BF16)
         return carry
 
     lax.fori_loop(0, tokens, place_token, 0)
@@ -178,8 +180,7 @@
         grad = rows[token_rows(token, pieces), :]
         total = jnp.zeros((pieces, LANES), F32)
         for k in range(top):
-            where = place[k, token]
-            row = returned[where >> 3, slot_rows(where & 7, pieces), :].astype(F32)
+            row = returned[slot_rows(place[k, token], pieces), :].astype(F32)
             total = total + weights[k, token] * row
             dots[k, pl.ds(token, 1), :] = jnp.sum(row * grad, axis=0, keepdims=True)
         sums[token_rows(token, pieces), :] = total
@@ -202,10 +203,10 @@
 
 
 def input_grad_kernel(
-    place_in, layer_in, inverse_in, gain_in, out_grad, returned, input_grad, gain_grad,
-    place, x, inverse, gain_rows, grad, held, units, sums, dots, result, in_sems, sems, out_sems,
+    place_in, x, inverse, gain_rows, grad, returned, input_grad, gain_grad,
+    place, held, extra, units, sums, dots, result, place_sem, sems, extra_sem, out_sems,
 ):
-    tokens, width = out_grad.shape
+    tokens, width = grad.shape
     pieces = width // LANES
     top = place.shape[0]
     peers = returned.shape[0]
@@ -213,23 +214,19 @@
     body_rows = returned.shape[1] - EXTRA
     parts = sems.shape[0]
     step = peers // parts
-    small = [
-        pltpu.make_async_copy(source, target, in_sems.at[i])
-        for i, (source, target) in enumerate(
-            ((layer_in, x), (inverse_in, inverse), (place_in, place), (gain_in, gain_rows), (out_grad, grad))
-        )
-    ]
-    for copy in small[:2]:
-        copy.start()
+    blocks = held.reshape(peers, body_rows, LANES)
     copies = []
     for i in range(parts):
         cut = pl.ds(i * step, step)
-        copies.append(pltpu.make_async_copy(returned.at[cut], held.at[cut], sems.at[i]))
-        copies[i].start()
-    for copy in small[2:]:
+        copies.append(
+            pltpu.make_async_copy(returned.at[cut, pl.ds(0, body_rows)], blocks.at[cut], sems.at[i])
+        )
+    copies.append(pltpu.make_async_copy(place_in, place, place_sem))
+    copies.append(
+        pltpu.make_async_copy(returned.at[:, pl.ds(body_rows, EXTRA)], extra, extra_sem)
+    )
+    for copy in copies:
         copy.start()
-    for copy in small[:2]:
-        copy.wait()
 
     def spread(group, carry):
         first = pl.multiple_of(group * GROUP, GROUP)
@@ -239,7 +236,7 @@
         return carry
 
     lax.fori_loop(0, tokens // GROUP, spread, 0)
-    for copy in small[2:] + copies:
+    for copy in copies:
         copy.wait()
 
     def combine(block, carry):
@@ -248,7 +245,7 @@
             wheres = [place[k, token] for k in range(top)]
             total = jnp.zeros((pieces, LANES), F32)
             for where in wheres:
-                total = total + held[where >> 3, slot_rows(where & 7, pieces), :].astype(F32)
+                total = total + held[slot_rows(where, pieces), :].astype(F32)
             q = total * gain_rows[...]
             sums[token_rows(token, pieces), :] = q
             along = q * units[token_rows(token, pieces), :]
@@ -256,8 +253,7 @@
         return carry
 
     lax.fori_loop(0, tokens // 4, combine, 0)
-    means = jnp.sum(dots[...], axis=-1, keepdims=True) / width
-    dots[...] = inverse[...] * means
+    dots[...] = inverse[...] * (jnp.sum(dots[...], axis=-1, keepdims=True) / width)
 
     def finish(group, carry):
         first = pl.multiple_of(group * GROUP, GROUP)
@@ -271,6 +267,11 @@
             ).astype(BF16)
         return carry
 
+    def add_peers(block, total):
+        for i in range(8):
+            total = total + extra[block * 8 + i].astype(F32)
+        return total
+
     out_parts = out_sems.shape[0]
     part = tokens // out_parts
     sent = []
@@ -279,12 +280,6 @@
         cut = pl.ds(i * part, part)
         sent.append(pltpu.make_async_copy(result.at[cut], input_grad.at[cut], out_sems.at[i]))
         sent[i].start()
-
-    def add_peers(block, total):
-        for i in range(8):
-            total = total + held[block * 8 + i, body_rows : body_rows + EXTRA, :].astype(F32)
-        return total
-
     total = lax.fori_loop(0, peers // 8, add_peers, jnp.zeros((EXTRA, LANES), F32))[0:1]
     gain_grad[...] = (
         total[:, :share] + total[:, share : 2 * share] + total[:, 2 * share : 3 * share]
@@ -343,7 +338,7 @@
             pltpu.VMEM((tokens, LANES), F32),
             pltpu.SMEM((top, tokens), jnp.int32),
             pltpu.SMEM((peers,), jnp.int32),
-            pltpu.SMEM((peers * 8,), jnp.int32),
+            pltpu.SMEM((row_count,), jnp.int32),
             pltpu.SemaphoreType.DMA((in_parts + 2,)),
             pltpu.SemaphoreType.DMA((out_parts + 2,)),
         ],
@@ -354,14 +349,14 @@
 
     send_grads = pl.pallas_call(
         send_grads_kernel,
-        out_shape=jax.ShapeDtypeStruct(block, BF16),
+        out_shape=jax.ShapeDtypeStruct((row_count * pieces, LANES), BF16),
         in_specs=[SMEM, SMEM, VMEM],
         out_specs=VMEM,
         scratch_shapes=[token_scratch],
         compiler_params=PARAMS,
         name="send_grads",
     )(place, weights, out_grad)
-    grad_rows = exchange(send_grads).reshape(row_count, pieces, LANES).reshape(row_count, width)
+    grad_rows = exchange(send_grads.reshape(block)).reshape(row_count, pieces, LANES).reshape(row_count, width)
 
     w_gate_up = expert_gate_up[0]
     w_down = expert_down[0]
@@ -402,9 +397,9 @@
         in_specs=[SMEM, SMEM, VMEM, VMEM, VMEM],
         out_specs=(VMEM, VMEM),
         scratch_shapes=[token_scratch, token_scratch, pltpu.VMEM((top, tokens, LANES), F32)],
-        compiler_params=PARAMS,
+        compiler_params=SMALL,
         name="outputs",
-    )(place, weights, layer_in, out_grad, returned)
+    )(place, weights, layer_in, out_grad, returned.reshape(row_count * pieces, LANES))
 
     input_grad, gain_grad = pl.pallas_call(
         input_grad_kernel,
@@ -412,24 +407,22 @@
             jax.ShapeDtypeStruct((tokens, width), BF16),
             jax.ShapeDtypeStruct((1, share), F32),
         ),
-        in_specs=[HBM] * 6,
+        in_specs=[HBM, VMEM, VMEM, VMEM, VMEM, HBM],
         out_specs=(HBM, VMEM),
         scratch_shapes=[
             pltpu.SMEM((top, tokens), jnp.int32),
-            pltpu.VMEM((tokens, width), BF16),
-            pltpu.VMEM((tokens, LANES), F32),
-            pltpu.VMEM((pieces, LANES), F32),
-            pltpu.VMEM((tokens, width), BF16),
-            pltpu.VMEM(came_back.shape, BF16),
+            pltpu.VMEM((row_count * pieces, LANES), BF16),
+            pltpu.VMEM((peers, EXTRA, LANES), BF16),
             token_scratch,
             token_scratch,
             pltpu.VMEM((tokens, LANES), F32),
             pltpu.VMEM((tokens, width), BF16),
-            pltpu.SemaphoreType.DMA((5,)),
+            pltpu.SemaphoreType.DMA(()),
             pltpu.SemaphoreType.DMA((8,)),
-            pltpu.SemaphoreType.DMA((4,)),
+            pltpu.SemaphoreType.DMA(()),
+            pltpu.SemaphoreType.DMA((8,)),
         ],
-        compiler_params=WHOLE,
+        compiler_params=SMALL,
         name="input_grad",
     )(place, layer_in, inverse, norm_gain.reshape(pieces, LANES), out_grad, came_back)
     gain_grad = gain_grad.reshape(share)

time: 304 us -> 302 us (level)
  no operation moved by 1% of the time
where the time goes in v3:
time: 302 us; the launch traced here: 301 us
  waiting for transfers between devices  151 us (50%)
  matrix products  46.4 us (15%)
  local copies, waits for them, and re-layouts  40.4 us (13%)
  starting transfers between devices  28.8 us (10%)
  Pallas kernels  27.3 us (9%)
  other arithmetic  5.41 us (2%)
    all_to_all x4, waiting for transfers between devices, exchange(): lax.all_to_all(buffer, ('dev', 'role'), split_axis=0, concat_axis=0, tile...  151 us
    all_to_all x4, starting transfers between devices, exchange(): lax.all_to_all(buffer, ('dev', 'role'), split_axis=0, concat_axis=0, tile...  28.8 us
    dot_general x2, matrix products, transposed(): lax.dot_general(left, right, (((1,), (1,)), ((), ())), preferred_element_...  27.8 us
    dot_general x1, matrix products, body(): projected = jnp.dot(arrived, w_gate_up, preferred_element_type=F32)  12.5 us
    pallas_call x1, Pallas kernels, body(): pl.pallas_call(outputs_kernel, out_shape=(jax.ShapeDtypeStruct((tokens, w...  9.57 us
    another operation x1, local copies, waits for them, and re-layouts, body(): exchange(send_rows).reshape(row_count, pieces, LANES)  8.98 us
    another operation x1, local copies, waits for them, and re-layouts, body(): back_rows.reshape(row_count, pieces, LANES).reshape(block)  8.91 us
    another operation x1, local copies, waits for them, and re-layouts, body(): expert_rows.reshape(row_count, pieces, LANES).reshape(block)  8.89 us
  transfers between devices with their start and end apart: 4, of which 4 were waited for; matrix products, arithmetic and copies ran while one was open for 29% of the time, Pallas kernels for 5%

profile of v3, /device:TPU:1, one launch (start us, length us, event | category | flops | bytes accessed | tf_op | source)
XLA Modules:
  0.0 300.7 jit_solution(13429862621799998601)
XLA Ops:
  0.6 6.2 %send_rows.1 = (bf16[128,160,128]{2,1,0:T(8,128)(2,1)}, s32[4,128]{1,0:T(4,128)}, f32[128,128]{1,0:T(8,128)}) custom-call(s32[4,128]{1,0:T(4,128)} %bitcast.47, bf16[128,4096]{1,0:T(8,128)(2,1)} %x.3, f32[1,4096]{1,0:T(1,128)} %bitcast.35), custom_call_target="tpu_custom_call" | custom-call | tf_op jit(solution)/shard_map/send_rows/pallas_call | solution.py:322
  6.8 0.0 copy-start.2
  6.8 0.0 copy-start.5
  6.9 0.0 copy-start.6
  6.9 11.9 %all-to-all-start = ((bf16[128,160,128]{2,1,0:T(8,128)(2,1)}), bf16[128,160,128]{2,1,0:T(8,128)(2,1)}, u32[]{:S(2)}, u32[]{:S(2)}) async-start(bf16[128,160,128]{2,1,0:T(8,128)(2,1)} %get-tuple-element.12), calls=%async_computation | async-start | bytes 10485760 | tf_op jit(solution)/shard_map/all_to_all | solution.py:296
  18.8 0.0 copy-done.2
  18.8 0.0 copy-done.5
  18.8 0.0 copy-done.6
  18.8 4.9 %send_grads.1 = bf16[20480,128]{1,0:T(8,128)(2,1)S(1)} custom-call(s32[4,128]{1,0:T(4,128)S(1)} %copy-done.5, f32[4,128]{1,0:T(4,128)S(1)} %bitcast.37, bf16[128,4096]{1,0:T(8,128)(2,1)S(1)} %copy-done.2), custom_call_target="tpu_custom_call" | custom-call | tf_op jit(solution)/shard_map/send_grads/pallas_call | solution.py:350
  23.7 0.0 copy-start
  23.7 2.4 copy-done
  26.1 56.4 %all-to-all-done = bf16[128,160,128]{2,1,0:T(8,128)(2,1)} async-done(((bf16[128,160,128]{2,1,0:T(8,128)(2,1)}), bf16[128,160,128]{2,1,0:T(8,128)(2,1)}, u32[]{:S(2)}, u32[]{:S(2)}) %all-to-all-start) | async-done | bytes 5242912 | tf_op jit(solution)/shard_map/all_to_all | solution.py:296
  82.5 5.6 %all-to-all-start.2 = ((bf16[128,160,128]{2,1,0:T(8,128)(2,1)}), bf16[128,160,128]{2,1,0:T(8,128)(2,1)}, u32[]{:S(2)}, u32[]{:S(2)}) async-start(bf16[128,160,128]{2,1,0:T(8,128)(2,1)} %bitcast.34), calls=%async_computation.2 | async-start | bytes 10485760 | tf_op jit(solution)/shard_map/all_to_all | solution.py:296
  88.2 0.0 slice-start.2
  88.2 9.0 %reshape_reshape.12 = bf16[640,4096]{1,0:T(8,128)(2,1)} reshape(bf16[128,160,128]{2,1,0:T(8,128)(2,1)} %all-to-all-done) | data formatting | bytes 10485760 | tf_op jit(solution)/shard_map/reshape;reshape | solution.py:348
  97.2 0.0 slice-start.3
  97.2 12.5 %fusion.2 = f32[640,1536]{1,0:T(8,128)S(1)} fusion(bf16[640,4096]{1,0:T(8,128)(2,1)} %reshape_reshape.12, bf16[1,4096,1536]{2,1,0:T(8,128)(2,1)} %param.12), kind=kOutput, calls=%fused_computation.2 | convolution fusion | flops 8053063680 | bytes 21757952 | tf_op jit(solution)/shard_map/dot_general | solution.py:363
  109.7 0.0 copy-start.7
  109.7 1.9 copy-done.7
  111.6 0.0 slice-done.2
  111.6 0.0 slice-done.3
  111.6 6.1 %convolution_convert_fusion = bf16[640,4096]{1,0:T(8,128)(2,1)} fusion(bf16[1,768,4096]{2,1,0:T(8,128)(2,1)S(1)} %bitcast.49, f32[640,1536]{1,0:T(8,128)S(1)} %fusion.2), kind=kOutput, calls=%fused_computation.8 | convolution fusion | flops 4032102400 | bytes 15466496 | tf_op jit(solution)/shard_map/dot_general | solution.py:369
  117.7 8.9 %reshape_reshape.13 = bf16[128,160,128]{2,1,0:T(8,128)(2,1)} reshape(bf16[640,4096]{1,0:T(8,128)(2,1)} %convolution_convert_fusion) | data formatting | bytes 10485760 | tf_op jit(solution)/shard_map/reshape;reshape | solution.py:370
  126.6 25.4 %all-to-all-done.2 = bf16[128,160,128]{2,1,0:T(8,128)(2,1)} async-done(((bf16[128,160,128]{2,1,0:T(8,128)(2,1)}), bf16[128,160,128]{2,1,0:T(8,128)(2,1)}, u32[]{:S(2)}, u32[]{:S(2)}) %all-to-all-start.2) | async-done | bytes 5242912 | tf_op jit(solution)/shard_map/all_to_all | solution.py:296
  152.1 5.6 %all-to-all-start.1 = ((bf16[128,160,128]{2,1,0:T(8,128)(2,1)}), bf16[128,160,128]{2,1,0:T(8,128)(2,1)}, u32[]{:S(2)}, u32[]{:S(2)}) async-start(bf16[128,160,128]{2,1,0:T(8,128)(2,1)} %reshape_reshape.13), calls=%async_computation.1 | async-start | bytes 10485760 | tf_op jit(solution)/shard_map/all_to_all | solution.py:296
  157.7 0.0 slice-start
  157.7 8.9 %reshape_reshape.14 = bf16[640,4096]{1,0:T(8,128)(2,1)} reshape(bf16[128,160,128]{2,1,0:T(8,128)(2,1)} %all-to-all-done.2) | data formatting | bytes 10485760 | tf_op jit(solution)/shard_map/reshape;reshape | solution.py:359
  166.6 10.3 %multiply_convert_fusion.1 = (bf16[640,768]{1,0:T(8,128)(2,1)S(1)}, bf16[640,768]{1,0:T(8,128)(2,1)S(1)}) fusion(f32[640,1536]{1,0:T(8,128)} %copy-done.7, bf16[640,4096]{1,0:T(8,128)(2,1)} %reshape_reshape.14, bf16[1,768,4096]{2,1,0:T(8,128)(2,1)} %param.13), kind=kOutput, calls=%fused_computation.17 | convolution fusion | flops 4032921600 | bytes 17432576 | tf_op jit(solution)/shard_map/dot_general | solution.py:292
  176.9 0.0 slice-done
  176.9 0.0 slice-done.1
  176.9 0.0 copy-start.3
  177.0 17.5 %multiply_reduce_fusion = (f32[4096]{0:T(1024)S(1)}, bf16[640,4096]{1,0:T(8,128)(2,1)}) fusion(bf16[640,4096]{1,0:T(8,128)(2,1)S(1)} %bitcast.40, bf16[1,4096,1536]{2,1,0:T(8,128)(2,1)} %param.12, bf16[640,768]{1,0:T(8,128)(2,1)S(1)} %get-tuple-element.19, bf16[640,768]{1,0:T(8,128)(2,1)S(1)} %get-tuple-element.18), kind=kOutput, calls=%fused_computation.6 | convolution fusion | flops 8070098944 | bytes 25051136 | tf_op jit(solution)/shard_map/dot_general | solution.py:292
  194.4 0.0 copy-done.3
  194.5 0.1 reshape.47
  194.6 0.1 reshape.49
  194.7 0.1 reshape.45
  194.8 0.1 maximum_bitcast_fusion
  194.9 0.1 copy.16
  195.0 8.9 %reshape_reshape.15 = bf16[128,160,128]{2,1,0:T(8,128)(2,1)} reshape(bf16[640,4096]{1,0:T(8,128)(2,1)} %get-tuple-element.24) | data formatting | bytes 10485760 | tf_op jit(solution)/shard_map/reshape;reshape | solution.py:387
  203.9 5.3 %fusion.11 = bf16[128,168,128]{2,1,0:T(8,128)(2,1)} fusion(bf16[128,1,96]{2,1,0:T(2,128)(2,1)S(1)} %copy.16, bf16[128,160,128]{2,1,0:T(8,128)(2,1)} %reshape_reshape.15), kind=kLoop, calls=%fused_computation.12 | loop fusion | flops 16515072 | bytes 10772480 | tf_op jit(solution)/shard_map/concatenate | solution.py:386
  209.2 12.4 %all-to-all-done.1 = bf16[128,160,128]{2,1,0:T(8,128)(2,1)} async-done(((bf16[128,160,128]{2,1,0:T(8,128)(2,1)}), bf16[128,160,128]{2,1,0:T(8,128)(2,1)}, u32[]{:S(2)}, u32[]{:S(2)}) %all-to-all-start.1) | async-done | bytes 5242912 | tf_op jit(solution)/shard_map/all_to_all | solution.py:296
  221.6 5.6 %all-to-all-start.3 = ((bf16[128,168,128]{2,1,0:T(8,128)(2,1)}), bf16[128,168,128]{2,1,0:T(8,128)(2,1)}, u32[]{:S(2)}, u32[]{:S(2)}) async-start(bf16[128,168,128]{2,1,0:T(8,128)(2,1)} %fusion.11), calls=%async_computation.3 | async-start | bytes 11010048 | tf_op jit(solution)/shard_map/all_to_all | solution.py:296
  227.2 0.0 copy-start.4
  227.2 0.0 copy-done.1
  227.3 9.6 %outputs.1 = (bf16[128,4096]{1,0:T(8,128)(2,1)}, f32[4,128]{1,0:T(4,128)}) custom-call(s32[4,128]{1,0:T(4,128)S(1)} %copy-done.5, f32[4,128]{1,0:T(4,128)S(1)} %bitcast.38, bf16[128,4096]{1,0:T(8,128)(2,1)S(1)} %copy-done.1, bf16[128,4096]{1,0:T(8,128)(2,1)S(1)} %copy-done.2, bf16[20480,128]{1,0:T(8,128)(2,1)} %bitcast.5.returned), custom_call_target="tpu_custom_call" | custom-call | tf_op jit(solution)/shard_map/outputs/pallas_call | solution.py:391
  236.8 57.1 %all-to-all-done.3.returned = bf16[128,168,128]{2,1,0:T(8,128)(2,1)} async-done(((bf16[128,168,128]{2,1,0:T(8,128)(2,1)}), bf16[128,168,128]{2,1,0:T(8,128)(2,1)}, u32[]{:S(2)}, u32[]{:S(2)}) %all-to-all-start.3) | async-done | bytes 5505056 | tf_op jit(solution)/shard_map/all_to_all | solution.py:296
  293.9 0.0 copy-done.4
  293.9 6.6 %input_grad.1 = (bf16[128,4096]{1,0:T(8,128)(2,1)}, f32[1,32]{1,0:T(1,128)}) custom-call(s32[4,128]{1,0:T(4,128)S(1)} %copy-done.5, bf16[128,4096]{1,0:T(8,128)(2,1)S(1)} %copy-done.1, f32[128,128]{1,0:T(8,128)S(1)} %copy-done.4, f32[32,128]{1,0:T(8,128)S(1)} %bitcast.36, bf16[128,4096]{1,0:T(8,128)(2,1)S(1)} %copy-done.2, ...), custom_call_target="tpu_custom_call" | custom-call | tf_op jit(solution)/shard_map/input_grad/pallas_call | solution.py:404
  (8 shorter events, 0.1 us)
Async XLA Ops:
  6.8 12.0 %copy-start.2 = (bf16[128,4096]{1,0:T(8,128)(2,1)S(1)}, bf16[128,4096]{1,0:T(8,128)(2,1)}, u32[]{:S(2)}) copy-start(bf16[128,4096]{1,0:T(8,128)(2,1)} %grad.1) | copy-start | bytes 3145732
  6.8 11.9 %copy-start.5 = (s32[4,128]{1,0:T(4,128)S(1)}, s32[4,128]{1,0:T(4,128)}, u32[]{:S(2)}) copy-start(s32[4,128]{1,0:T(4,128)} %get-tuple-element.11.place.place_in) | copy-start | bytes 6148
  6.9 11.9 %copy-start.6 = (f32[128,4]{0,1:T(4,128)S(1)}, f32[128,4]{0,1:T(4,128)}, u32[]{:S(2)}) copy-start(f32[128,4]{0,1:T(4,128)} %param.10) | copy-start | bytes 6148
  6.9 75.7 %all-to-all-start = ((bf16[128,160,128]{2,1,0:T(8,128)(2,1)}), bf16[128,160,128]{2,1,0:T(8,128)(2,1)}, u32[]{:S(2)}, u32[]{:S(2)}) async-start(bf16[128,160,128]{2,1,0:T(8,128)(2,1)} %get-tuple-element.12), calls=%async_computation | async-start | bytes 10485760 | tf_op jit(solution)/shard_map/all_to_all | solution.py:296
  23.7 2.4 copy-start
  82.5 69.5 %all-to-all-start.2 = ((bf16[128,160,128]{2,1,0:T(8,128)(2,1)}), bf16[128,160,128]{2,1,0:T(8,128)(2,1)}, u32[]{:S(2)}, u32[]{:S(2)}) async-start(bf16[128,160,128]{2,1,0:T(8,128)(2,1)} %bitcast.34), calls=%async_computation.2 | async-start | bytes 10485760 | tf_op jit(solution)/shard_map/all_to_all | solution.py:296
  88.2 23.4 %slice-start.2 = ((s8[6291456]{0:T(1024)(128)(4,1)}), s8[2097152]{0:T(1024)(128)(4,1)S(1)}, s32[]{:S(2)}) async-start(s8[6291456]{0:T(1024)(128)(4,1)} %bitcast.48), calls=%async_computation.6 | async-start | bytes 4194304
  97.2 14.4 %slice-start.3 = ((s8[6291456]{0:T(1024)(128)(4,1)}), s8[4194304]{0:T(1024)(128)(4,1)S(1)}, s32[]{:S(2)}) async-start(s8[6291456]{0:T(1024)(128)(4,1)} %bitcast.48), calls=%async_computation.7 | async-start | bytes 8388608
  109.7 1.9 copy-start.7
  152.1 69.5 %all-to-all-start.1 = ((bf16[128,160,128]{2,1,0:T(8,128)(2,1)}), bf16[128,160,128]{2,1,0:T(8,128)(2,1)}, u32[]{:S(2)}, u32[]{:S(2)}) async-start(bf16[128,160,128]{2,1,0:T(8,128)(2,1)} %reshape_reshape.13), calls=%async_computation.1 | async-start | bytes 10485760 | tf_op jit(solution)/shard_map/all_to_all | solution.py:296
  157.7 19.2 %slice-start = ((s8[5242880]{0:T(1024)(128)(4,1)}), s8[1048576]{0:T(1024)(128)(4,1)S(1)}, s32[]{:S(2)}) async-start(s8[5242880]{0:T(1024)(128)(4,1)} %bitcast.39), calls=%async_computation.4 | async-start | bytes 2097152
  166.6 10.3 %slice-start.1 = ((s8[5242880]{0:T(1024)(128)(4,1)}), s8[4194304]{0:T(1024)(128)(4,1)S(1)}, s32[]{:S(2)}) async-start(s8[5242880]{0:T(1024)(128)(4,1)} %bitcast.39), calls=%async_computation.5 | async-start | bytes 8388608
  176.9 17.5 %copy-start.3 = (f32[4096]{0:T(1024)S(1)}, f32[4096]{0:T(1024)}, u32[]{:S(2)}) copy-start(f32[4096]{0:T(1024)} %param.8) | copy-start | bytes 49156
  209.2 18.0 %copy-start.1 = (bf16[128,4096]{1,0:T(8,128)(2,1)S(1)}, bf16[128,4096]{1,0:T(8,128)(2,1)}, u32[]{:S(2)}) copy-start(bf16[128,4096]{1,0:T(8,128)(2,1)} %x.3) | copy-start | bytes 3145732
  221.6 72.3 %all-to-all-start.3 = ((bf16[128,168,128]{2,1,0:T(8,128)(2,1)}), bf16[128,168,128]{2,1,0:T(8,128)(2,1)}, u32[]{:S(2)}, u32[]{:S(2)}) async-start(bf16[128,168,128]{2,1,0:T(8,128)(2,1)} %fusion.11), calls=%async_computation.3 | async-start | bytes 11010048 | tf_op jit(solution)/shard_map/all_to_all | solution.py:296
  227.2 66.7 %copy-start.4 = (f32[128,128]{1,0:T(8,128)S(1)}, f32[128,128]{1,0:T(8,128)}, u32[]{:S(2)}) copy-start(f32[128,128]{1,0:T(8,128)} %get-tuple-element.14.inverse) | copy-start | bytes 196612

commit v4 on v3

--- a/solution.py
+++ b/solution.py
@@ -11,7 +11,7 @@
 EPSILON = 1e-06
 LANES = 128
 GROUP = 16
-EXTRA = 8
+PAIR = 2
 F32 = jnp.float32
 BF16 = jnp.bfloat16
 VMEM = pl.BlockSpec(memory_space=pltpu.VMEM)
@@ -209,9 +209,10 @@
     tokens, width = grad.shape
     pieces = width // LANES
     top = place.shape[0]
-    peers = returned.shape[0]
+    peers, pairs = returned.shape[:2]
     share = gain_grad.shape[1]
-    body_rows = returned.shape[1] - EXTRA
+    body_rows = (pairs - 1) * PAIR
+    arrived = returned.reshape(peers, pairs * PAIR, LANES)
     parts = sems.shape[0]
     step = peers // parts
     blocks = held.reshape(peers, body_rows, LANES)
@@ -219,12 +220,10 @@
     for i in range(parts):
         cut = pl.ds(i * step, step)
         copies.append(
-            pltpu.make_async_copy(returned.at[cut, pl.ds(0, body_rows)], blocks.at[cut], sems.at[i])
+            pltpu.make_async_copy(arrived.at[cut, pl.ds(0, body_rows)], blocks.at[cut], sems.at[i])
         )
     copies.append(pltpu.make_async_copy(place_in, place, place_sem))
-    copies.append(
-        pltpu.make_async_copy(returned.at[:, pl.ds(body_rows, EXTRA)], extra, extra_sem)
-    )
+    copies.append(pltpu.make_async_copy(returned.at[:, pl.ds(pairs - 1, 1)], extra, extra_sem))
     for copy in copies:
         copy.start()
 
@@ -269,7 +268,7 @@
 
     def add_peers(block, total):
         for i in range(8):
-            total = total + extra[block * 8 + i].astype(F32)
+            total = total + extra[block * 8 + i, 0].astype(F32)
         return total
 
     out_parts = out_sems.shape[0]
@@ -280,7 +279,7 @@
         cut = pl.ds(i * part, part)
         sent.append(pltpu.make_async_copy(result.at[cut], input_grad.at[cut], out_sems.at[i]))
         sent[i].start()
-    total = lax.fori_loop(0, peers // 8, add_peers, jnp.zeros((EXTRA, LANES), F32))[0:1]
+    total = lax.fori_loop(0, peers // 8, add_peers, jnp.zeros((PAIR, LANES), F32))[0:1]
     gain_grad[...] = (
         total[:, :share] + total[:, share : 2 * share] + total[:, 2 * share : 3 * share]
     )
@@ -382,10 +381,9 @@
         ],
         axis=-1,
     )
-    parts = jnp.pad(parts[:, None, :], ((0, 0), (0, EXTRA - 1), (0, LANES - 3 * share)))
-    send_back = jnp.concatenate(
-        [back_rows.reshape(row_count, pieces, LANES).reshape(block), parts], axis=1
-    )
+    parts = jnp.pad(parts[:, None, None, :], ((0, 0), (0, 0), (0, PAIR - 1), (0, LANES - 3 * share)))
+    back_pairs = back_rows.reshape(row_count, pieces, LANES).reshape(peers, -1, PAIR, LANES)
+    send_back = jnp.concatenate([back_pairs, parts], axis=1)
     came_back = exchange(send_back)
 
     layer_out, gate_grad = pl.pallas_call(
@@ -412,7 +410,7 @@
         scratch_shapes=[
             pltpu.SMEM((top, tokens), jnp.int32),
             pltpu.VMEM((row_count * pieces, LANES), BF16),
-            pltpu.VMEM((peers, EXTRA, LANES), BF16),
+            pltpu.VMEM((peers, 1, PAIR, LANES), BF16),
             token_scratch,
             token_scratch,
             pltpu.VMEM((tokens, LANES), F32),

time: 302 us -> 300 us (level)
  waiting for transfers between devices: 151 us -> 147 us
    all_to_all x4, waiting for transfers between devices: 151 us -> 147 us  [exchange(): lax.all_to_all(buffer, ('dev', 'role'), split_axis=0, concat_axis=0, tile...]
  transfers between devices with their start and end apart: 4 -> 4, of which waited for: 4 -> 4; matrix products, arithmetic and copies ran while one was open for 29% -> 30% of each run, Pallas kernels for 5% -> 5%
where the time goes in v4:
time: 300 us; the launch traced here: 299 us
  waiting for transfers between devices  147 us (49%)
  matrix products  46.4 us (15%)
  local copies, waits for them, and re-layouts  40.8 us (14%)
  starting transfers between devices  28.8 us (10%)
  Pallas kernels  27.3 us (9%)
  other arithmetic  7.06 us (2%)
    all_to_all x4, waiting for transfers between devices, exchange(): lax.all_to_all(buffer, ('dev', 'role'), split_axis=0, concat_axis=0, tile...  147 us
    all_to_all x4, starting transfers between devices, exchange(): lax.all_to_all(buffer, ('dev', 'role'), split_axis=0, concat_axis=0, tile...  28.8 us
    dot_general x2, matrix products, transposed(): lax.dot_general(left, right, (((1,), (1,)), ((), ())), preferred_element_...  27.8 us
    dot_general x1, matrix products, body(): projected = jnp.dot(arrived, w_gate_up, preferred_element_type=F32)  12.5 us
    pallas_call x1, Pallas kernels, body(): pl.pallas_call(outputs_kernel, out_shape=(jax.ShapeDtypeStruct((tokens, w...  9.57 us
    another operation x1, local copies, waits for them, and re-layouts, body(): back_rows.reshape(row_count, pieces, LANES).reshape(peers, -1, PAIR, LANES)  9.34 us
    another operation x1, local copies, waits for them, and re-layouts, body(): exchange(send_rows).reshape(row_count, pieces, LANES)  8.98 us
    another operation x1, local copies, waits for them, and re-layouts, body(): expert_rows.reshape(row_count, pieces, LANES).reshape(block)  8.89 us
  transfers between devices with their start and end apart: 4, of which 4 were waited for; matrix products, arithmetic and copies ran while one was open for 30% of the time, Pallas kernels for 5%

profile of v4, /device:TPU:1, one launch (start us, length us, event | category | flops | bytes accessed | tf_op | source)
XLA Modules:
  0.0 298.6 jit_solution(8855896749830286830)
XLA Ops:
  0.6 6.2 %send_rows.1 = (bf16[128,160,128]{2,1,0:T(8,128)(2,1)}, s32[4,128]{1,0:T(4,128)}, f32[128,128]{1,0:T(8,128)}) custom-call(s32[4,128]{1,0:T(4,128)} %bitcast.47, bf16[128,4096]{1,0:T(8,128)(2,1)} %x.3, f32[1,4096]{1,0:T(1,128)} %bitcast.35), custom_call_target="tpu_custom_call" | custom-call | tf_op jit(solution)/shard_map/send_rows/pallas_call | solution.py:321
  6.8 0.0 copy-start.2
  6.8 0.0 copy-start.5
  6.9 0.0 copy-start.6
  6.9 11.9 %all-to-all-start = ((bf16[128,160,128]{2,1,0:T(8,128)(2,1)}), bf16[128,160,128]{2,1,0:T(8,128)(2,1)}, u32[]{:S(2)}, u32[]{:S(2)}) async-start(bf16[128,160,128]{2,1,0:T(8,128)(2,1)} %get-tuple-element.12), calls=%async_computation | async-start | bytes 10485760 | tf_op jit(solution)/shard_map/all_to_all | solution.py:295
  18.8 0.0 copy-done.2
  18.8 0.0 copy-done.5
  18.8 0.0 copy-done.6
  18.8 4.9 %send_grads.1 = bf16[20480,128]{1,0:T(8,128)(2,1)S(1)} custom-call(s32[4,128]{1,0:T(4,128)S(1)} %copy-done.5, f32[4,128]{1,0:T(4,128)S(1)} %bitcast.37, bf16[128,4096]{1,0:T(8,128)(2,1)S(1)} %copy-done.2), custom_call_target="tpu_custom_call" | custom-call | tf_op jit(solution)/shard_map/send_grads/pallas_call | solution.py:349
  23.7 0.0 copy-start
  23.7 2.4 copy-done
  26.1 56.4 %all-to-all-done = bf16[128,160,128]{2,1,0:T(8,128)(2,1)} async-done(((bf16[128,160,128]{2,1,0:T(8,128)(2,1)}), bf16[128,160,128]{2,1,0:T(8,128)(2,1)}, u32[]{:S(2)}, u32[]{:S(2)}) %all-to-all-start) | async-done | bytes 5242912 | tf_op jit(solution)/shard_map/all_to_all | solution.py:295
  82.5 5.6 %all-to-all-start.2 = ((bf16[128,160,128]{2,1,0:T(8,128)(2,1)}), bf16[128,160,128]{2,1,0:T(8,128)(2,1)}, u32[]{:S(2)}, u32[]{:S(2)}) async-start(bf16[128,160,128]{2,1,0:T(8,128)(2,1)} %bitcast.34), calls=%async_computation.2 | async-start | bytes 10485760 | tf_op jit(solution)/shard_map/all_to_all | solution.py:295
  88.2 0.0 slice-start.2
  88.2 9.0 %reshape_reshape.12 = bf16[640,4096]{1,0:T(8,128)(2,1)} reshape(bf16[128,160,128]{2,1,0:T(8,128)(2,1)} %all-to-all-done) | data formatting | bytes 10485760 | tf_op jit(solution)/shard_map/reshape;reshape | solution.py:347
  97.2 0.0 slice-start.3
  97.2 12.5 %fusion.2 = f32[640,1536]{1,0:T(8,128)S(1)} fusion(bf16[640,4096]{1,0:T(8,128)(2,1)} %reshape_reshape.12, bf16[1,4096,1536]{2,1,0:T(8,128)(2,1)} %param.12), kind=kOutput, calls=%fused_computation.3 | convolution fusion | flops 8053063680 | bytes 21757952 | tf_op jit(solution)/shard_map/dot_general | solution.py:362
  109.7 0.0 copy-start.7
  109.7 1.9 copy-done.7
  111.6 0.0 slice-done.2
  111.6 0.0 slice-done.3
  111.6 6.1 %convolution_convert_fusion = bf16[640,4096]{1,0:T(8,128)(2,1)} fusion(bf16[1,768,4096]{2,1,0:T(8,128)(2,1)S(1)} %bitcast.49, f32[640,1536]{1,0:T(8,128)S(1)} %fusion.2), kind=kOutput, calls=%fused_computation.7 | convolution fusion | flops 4032102400 | bytes 15466496 | tf_op jit(solution)/shard_map/dot_general | solution.py:368
  117.7 8.9 %reshape_reshape.13 = bf16[128,160,128]{2,1,0:T(8,128)(2,1)} reshape(bf16[640,4096]{1,0:T(8,128)(2,1)} %convolution_convert_fusion) | data formatting | bytes 10485760 | tf_op jit(solution)/shard_map/reshape;reshape | solution.py:369
  126.6 25.4 %all-to-all-done.2 = bf16[128,160,128]{2,1,0:T(8,128)(2,1)} async-done(((bf16[128,160,128]{2,1,0:T(8,128)(2,1)}), bf16[128,160,128]{2,1,0:T(8,128)(2,1)}, u32[]{:S(2)}, u32[]{:S(2)}) %all-to-all-start.2) | async-done | bytes 5242912 | tf_op jit(solution)/shard_map/all_to_all | solution.py:295
  152.1 5.6 %all-to-all-start.1 = ((bf16[128,160,128]{2,1,0:T(8,128)(2,1)}), bf16[128,160,128]{2,1,0:T(8,128)(2,1)}, u32[]{:S(2)}, u32[]{:S(2)}) async-start(bf16[128,160,128]{2,1,0:T(8,128)(2,1)} %reshape_reshape.13), calls=%async_computation.1 | async-start | bytes 10485760 | tf_op jit(solution)/shard_map/all_to_all | solution.py:295
  157.7 0.0 slice-start
  157.7 8.9 %reshape_reshape.14 = bf16[640,4096]{1,0:T(8,128)(2,1)} reshape(bf16[128,160,128]{2,1,0:T(8,128)(2,1)} %all-to-all-done.2) | data formatting | bytes 10485760 | tf_op jit(solution)/shard_map/reshape;reshape | solution.py:358
  166.6 10.3 %multiply_convert_fusion.1 = (bf16[640,768]{1,0:T(8,128)(2,1)S(1)}, bf16[640,768]{1,0:T(8,128)(2,1)S(1)}) fusion(f32[640,1536]{1,0:T(8,128)} %copy-done.7, bf16[640,4096]{1,0:T(8,128)(2,1)} %reshape_reshape.14, bf16[1,768,4096]{2,1,0:T(8,128)(2,1)} %param.13), kind=kOutput, calls=%fused_computation.16 | convolution fusion | flops 4032921600 | bytes 17432576 | tf_op jit(solution)/shard_map/dot_general | solution.py:291
  176.9 0.0 slice-done
  176.9 0.0 slice-done.1
  176.9 0.0 copy-start.3
  177.0 17.5 %multiply_reduce_fusion = (f32[4096]{0:T(1024)S(1)}, bf16[640,4096]{1,0:T(8,128)(2,1)}) fusion(bf16[640,4096]{1,0:T(8,128)(2,1)S(1)} %bitcast.40, bf16[1,4096,1536]{2,1,0:T(8,128)(2,1)} %param.12, bf16[640,768]{1,0:T(8,128)(2,1)S(1)} %get-tuple-element.19, bf16[640,768]{1,0:T(8,128)(2,1)S(1)} %get-tuple-element.18), kind=kOutput, calls=%fused_computation.5 | convolution fusion | flops 8070098944 | bytes 25051136 | tf_op jit(solution)/shard_map/dot_general | solution.py:291
  194.4 0.0 copy-done.3
  194.5 0.1 reshape.47
  194.6 0.1 reshape.49
  194.7 0.1 reshape.45
  194.8 0.1 maximum_bitcast_fusion
  194.9 0.1 copy.16
  195.0 9.3 %reshape_reshape.15 = bf16[128,80,2,128]{3,2,1,0:T(2,128)(2,1)} reshape(bf16[640,4096]{1,0:T(8,128)(2,1)} %get-tuple-element.24) | data formatting | bytes 10485760 | tf_op jit(solution)/shard_map/reshape;reshape | solution.py:385
  204.3 7.0 %fusion.10 = bf16[128,81,2,128]{3,2,1,0:T(2,128)(2,1)} fusion(bf16[128,1,1,96]{3,2,1,0:T(2,128)(2,1)S(1)} %copy.16, bf16[128,80,2,128]{3,2,1,0:T(2,128)(2,1)} %reshape_reshape.15), kind=kLoop, calls=%fused_computation.11 | loop fusion | flops 15925248 | bytes 10575872 | tf_op jit(solution)/shard_map/concatenate | solution.py:386
  211.3 10.3 %all-to-all-done.1 = bf16[128,160,128]{2,1,0:T(8,128)(2,1)} async-done(((bf16[128,160,128]{2,1,0:T(8,128)(2,1)}), bf16[128,160,128]{2,1,0:T(8,128)(2,1)}, u32[]{:S(2)}, u32[]{:S(2)}) %all-to-all-start.1) | async-done | bytes 5242912 | tf_op jit(solution)/shard_map/all_to_all | solution.py:295
  221.6 5.6 %all-to-all-start.3 = ((bf16[128,81,2,128]{3,2,1,0:T(2,128)(2,1)}), bf16[128,81,2,128]{3,2,1,0:T(2,128)(2,1)}, u32[]{:S(2)}, u32[]{:S(2)}) async-start(bf16[128,81,2,128]{3,2,1,0:T(2,128)(2,1)} %fusion.10), calls=%async_computation.3 | async-start | bytes 10616832 | tf_op jit(solution)/shard_map/all_to_all | solution.py:295
  227.2 0.0 copy-start.4
  227.2 0.0 copy-done.1
  227.3 9.6 %outputs.1 = (bf16[128,4096]{1,0:T(8,128)(2,1)}, f32[4,128]{1,0:T(4,128)}) custom-call(s32[4,128]{1,0:T(4,128)S(1)} %copy-done.5, f32[4,128]{1,0:T(4,128)S(1)} %bitcast.38, bf16[128,4096]{1,0:T(8,128)(2,1)S(1)} %copy-done.1, bf16[128,4096]{1,0:T(8,128)(2,1)S(1)} %copy-done.2, bf16[20480,128]{1,0:T(8,128)(2,1)} %bitcast.5.returned), custom_call_target="tpu_custom_call" | custom-call | tf_op jit(solution)/shard_map/outputs/pallas_call | solution.py:389
  236.8 55.0 %all-to-all-done.3.returned = bf16[128,81,2,128]{3,2,1,0:T(2,128)(2,1)} async-done(((bf16[128,81,2,128]{3,2,1,0:T(2,128)(2,1)}), bf16[128,81,2,128]{3,2,1,0:T(2,128)(2,1)}, u32[]{:S(2)}, u32[]{:S(2)}) %all-to-all-start.3) | async-done | bytes 5308448 | tf_op jit(solution)/shard_map/all_to_all | solution.py:295
  291.8 0.0 copy-done.4
  291.8 6.6 %input_grad.1 = (bf16[128,4096]{1,0:T(8,128)(2,1)}, f32[1,32]{1,0:T(1,128)}) custom-call(s32[4,128]{1,0:T(4,128)S(1)} %copy-done.5, bf16[128,4096]{1,0:T(8,128)(2,1)S(1)} %copy-done.1, f32[128,128]{1,0:T(8,128)S(1)} %copy-done.4, f32[32,128]{1,0:T(8,128)S(1)} %bitcast.36, bf16[128,4096]{1,0:T(8,128)(2,1)S(1)} %copy-done.2, ...), custom_call_target="tpu_custom_call" | custom-call | tf_op jit(solution)/shard_map/input_grad/pallas_call | solution.py:402
  (8 shorter events, 0.1 us)
Async XLA Ops:
  6.8 12.0 %copy-start.2 = (bf16[128,4096]{1,0:T(8,128)(2,1)S(1)}, bf16[128,4096]{1,0:T(8,128)(2,1)}, u32[]{:S(2)}) copy-start(bf16[128,4096]{1,0:T(8,128)(2,1)} %grad.1) | copy-start | bytes 3145732
  6.8 11.9 %copy-start.5 = (s32[4,128]{1,0:T(4,128)S(1)}, s32[4,128]{1,0:T(4,128)}, u32[]{:S(2)}) copy-start(s32[4,128]{1,0:T(4,128)} %get-tuple-element.11.place.place_in) | copy-start | bytes 6148
  6.9 11.9 %copy-start.6 = (f32[128,4]{0,1:T(4,128)S(1)}, f32[128,4]{0,1:T(4,128)}, u32[]{:S(2)}) copy-start(f32[128,4]{0,1:T(4,128)} %param.10) | copy-start | bytes 6148
  6.9 75.7 %all-to-all-start = ((bf16[128,160,128]{2,1,0:T(8,128)(2,1)}), bf16[128,160,128]{2,1,0:T(8,128)(2,1)}, u32[]{:S(2)}, u32[]{:S(2)}) async-start(bf16[128,160,128]{2,1,0:T(8,128)(2,1)} %get-tuple-element.12), calls=%async_computation | async-start | bytes 10485760 | tf_op jit(solution)/shard_map/all_to_all | solution.py:295
  23.7 2.4 copy-start
  82.5 69.5 %all-to-all-start.2 = ((bf16[128,160,128]{2,1,0:T(8,128)(2,1)}), bf16[128,160,128]{2,1,0:T(8,128)(2,1)}, u32[]{:S(2)}, u32[]{:S(2)}) async-start(bf16[128,160,128]{2,1,0:T(8,128)(2,1)} %bitcast.34), calls=%async_computation.2 | async-start | bytes 10485760 | tf_op jit(solution)/shard_map/all_to_all | solution.py:295
  88.2 23.4 %slice-start.2 = ((s8[6291456]{0:T(1024)(128)(4,1)}), s8[2097152]{0:T(1024)(128)(4,1)S(1)}, s32[]{:S(2)}) async-start(s8[6291456]{0:T(1024)(128)(4,1)} %bitcast.48), calls=%async_computation.6 | async-start | bytes 4194304
  97.2 14.4 %slice-start.3 = ((s8[6291456]{0:T(1024)(128)(4,1)}), s8[4194304]{0:T(1024)(128)(4,1)S(1)}, s32[]{:S(2)}) async-start(s8[6291456]{0:T(1024)(128)(4,1)} %bitcast.48), calls=%async_computation.7 | async-start | bytes 8388608
  109.7 1.9 copy-start.7
  152.1 69.5 %all-to-all-start.1 = ((bf16[128,160,128]{2,1,0:T(8,128)(2,1)}), bf16[128,160,128]{2,1,0:T(8,128)(2,1)}, u32[]{:S(2)}, u32[]{:S(2)}) async-start(bf16[128,160,128]{2,1,0:T(8,128)(2,1)} %reshape_reshape.13), calls=%async_computation.1 | async-start | bytes 10485760 | tf_op jit(solution)/shard_map/all_to_all | solution.py:295
  157.7 19.2 %slice-start = ((s8[5242880]{0:T(1024)(128)(4,1)}), s8[1048576]{0:T(1024)(128)(4,1)S(1)}, s32[]{:S(2)}) async-start(s8[5242880]{0:T(1024)(128)(4,1)} %bitcast.39), calls=%async_computation.4 | async-start | bytes 2097152
  166.6 10.3 %slice-start.1 = ((s8[5242880]{0:T(1024)(128)(4,1)}), s8[4194304]{0:T(1024)(128)(4,1)S(1)}, s32[]{:S(2)}) async-start(s8[5242880]{0:T(1024)(128)(4,1)} %bitcast.39), calls=%async_computation.5 | async-start | bytes 8388608
  176.9 17.5 %copy-start.3 = (f32[4096]{0:T(1024)S(1)}, f32[4096]{0:T(1024)}, u32[]{:S(2)}) copy-start(f32[4096]{0:T(1024)} %param.8) | copy-start | bytes 49156
  211.3 15.9 %copy-start.1 = (bf16[128,4096]{1,0:T(8,128)(2,1)S(1)}, bf16[128,4096]{1,0:T(8,128)(2,1)}, u32[]{:S(2)}) copy-start(bf16[128,4096]{1,0:T(8,128)(2,1)} %x.3) | copy-start | bytes 3145732
  221.6 70.2 %all-to-all-start.3 = ((bf16[128,81,2,128]{3,2,1,0:T(2,128)(2,1)}), bf16[128,81,2,128]{3,2,1,0:T(2,128)(2,1)}, u32[]{:S(2)}, u32[]{:S(2)}) async-start(bf16[128,81,2,128]{3,2,1,0:T(2,128)(2,1)} %fusion.10), calls=%async_computation.3 | async-start | bytes 10616832 | tf_op jit(solution)/shard_map/all_to_all | solution.py:295
  227.2 64.6 %copy-start.4 = (f32[128,128]{1,0:T(8,128)S(1)}, f32[128,128]{1,0:T(8,128)}, u32[]{:S(2)}) copy-start(f32[128,128]{1,0:T(8,128)} %get-tuple-element.14.inverse) | copy-start | bytes 196612

commit v5 on v4

--- a/solution.py
+++ b/solution.py
@@ -239,8 +239,8 @@
         copy.wait()
 
     def combine(block, carry):
-        for i in range(4):
-            token = block * 4 + i
+        for i in range(8):
+            token = block * 8 + i
             wheres = [place[k, token] for k in range(top)]
             total = jnp.zeros((pieces, LANES), F32)
             for where in wheres:
@@ -251,7 +251,7 @@
             dots[pl.ds(token, 1), :] = jnp.sum(along, axis=0, keepdims=True)
         return carry
 
-    lax.fori_loop(0, tokens // 4, combine, 0)
+    lax.fori_loop(0, tokens // 8, combine, 0)
     dots[...] = inverse[...] * (jnp.sum(dots[...], axis=-1, keepdims=True) / width)
 
     def finish(group, carry):

time: 300 us -> 300 us (level)
  no operation moved by 1% of the time
where the time goes in v5:
time: 300 us; the launch traced here: 298 us
  waiting for transfers between devices  147 us (49%)
  matrix products  46.4 us (15%)
  local copies, waits for them, and re-layouts  40.8 us (14%)
  starting transfers between devices  28.8 us (10%)
  Pallas kernels  27 us (9%)
  other arithmetic  7.06 us (2%)
    all_to_all x4, waiting for transfers between devices, exchange(): lax.all_to_all(buffer, ('dev', 'role'), split_axis=0, concat_axis=0, tile...  147 us
    all_to_all x4, starting transfers between devices, exchange(): lax.all_to_all(buffer, ('dev', 'role'), split_axis=0, concat_axis=0, tile...  28.8 us
    dot_general x2, matrix products, transposed(): lax.dot_general(left, right, (((1,), (1,)), ((), ())), preferred_element_...  27.8 us
    dot_general x1, matrix products, body(): projected = jnp.dot(arrived, w_gate_up, preferred_element_type=F32)  12.5 us
    pallas_call x1, Pallas kernels, body(): pl.pallas_call(outputs_kernel, out_shape=(jax.ShapeDtypeStruct((tokens, w...  9.57 us
    another operation x1, local copies, waits for them, and re-layouts, body(): back_rows.reshape(row_count, pieces, LANES).reshape(peers, -1, PAIR, LANES)  9.34 us
    another operation x1, local copies, waits for them, and re-layouts, body(): exchange(send_rows).reshape(row_count, pieces, LANES)  8.98 us
    another operation x1, local copies, waits for them, and re-layouts, body(): expert_rows.reshape(row_count, pieces, LANES).reshape(block)  8.89 us
  transfers between devices with their start and end apart: 4, of which 4 were waited for; matrix products, arithmetic and copies ran while one was open for 30% of the time, Pallas kernels for 5%

profile of v5, /device:TPU:1, one launch (start us, length us, event | category | flops | bytes accessed | tf_op | source)
XLA Modules:
  0.0 298.3 jit_solution(11360367901931636507)
XLA Ops:
  0.6 6.2 %send_rows.1 = (bf16[128,160,128]{2,1,0:T(8,128)(2,1)}, s32[4,128]{1,0:T(4,128)}, f32[128,128]{1,0:T(8,128)}) custom-call(s32[4,128]{1,0:T(4,128)} %bitcast.47, bf16[128,4096]{1,0:T(8,128)(2,1)} %x.3, f32[1,4096]{1,0:T(1,128)} %bitcast.35), custom_call_target="tpu_custom_call" | custom-call | tf_op jit(solution)/shard_map/send_rows/pallas_call | solution.py:321
  6.8 0.0 copy-start.2
  6.8 0.0 copy-start.5
  6.9 0.0 copy-start.6
  6.9 11.9 %all-to-all-start = ((bf16[128,160,128]{2,1,0:T(8,128)(2,1)}), bf16[128,160,128]{2,1,0:T(8,128)(2,1)}, u32[]{:S(2)}, u32[]{:S(2)}) async-start(bf16[128,160,128]{2,1,0:T(8,128)(2,1)} %get-tuple-element.12), calls=%async_computation | async-start | bytes 10485760 | tf_op jit(solution)/shard_map/all_to_all | solution.py:295
  18.8 0.0 copy-done.2
  18.8 0.0 copy-done.5
  18.8 0.0 copy-done.6
  18.8 4.9 %send_grads.1 = bf16[20480,128]{1,0:T(8,128)(2,1)S(1)} custom-call(s32[4,128]{1,0:T(4,128)S(1)} %copy-done.5, f32[4,128]{1,0:T(4,128)S(1)} %bitcast.37, bf16[128,4096]{1,0:T(8,128)(2,1)S(1)} %copy-done.2), custom_call_target="tpu_custom_call" | custom-call | tf_op jit(solution)/shard_map/send_grads/pallas_call | solution.py:349
  23.7 0.0 copy-start
  23.7 2.4 copy-done
  26.1 56.4 %all-to-all-done = bf16[128,160,128]{2,1,0:T(8,128)(2,1)} async-done(((bf16[128,160,128]{2,1,0:T(8,128)(2,1)}), bf16[128,160,128]{2,1,0:T(8,128)(2,1)}, u32[]{:S(2)}, u32[]{:S(2)}) %all-to-all-start) | async-done | bytes 5242912 | tf_op jit(solution)/shard_map/all_to_all | solution.py:295
  82.5 5.6 %all-to-all-start.2 = ((bf16[128,160,128]{2,1,0:T(8,128)(2,1)}), bf16[128,160,128]{2,1,0:T(8,128)(2,1)}, u32[]{:S(2)}, u32[]{:S(2)}) async-start(bf16[128,160,128]{2,1,0:T(8,128)(2,1)} %bitcast.34), calls=%async_computation.2 | async-start | bytes 10485760 | tf_op jit(solution)/shard_map/all_to_all | solution.py:295
  88.2 0.0 slice-start.2
  88.2 9.0 %reshape_reshape.12 = bf16[640,4096]{1,0:T(8,128)(2,1)} reshape(bf16[128,160,128]{2,1,0:T(8,128)(2,1)} %all-to-all-done) | data formatting | bytes 10485760 | tf_op jit(solution)/shard_map/reshape;reshape | solution.py:347
  97.2 0.0 slice-start.3
  97.2 12.5 %fusion.2 = f32[640,1536]{1,0:T(8,128)S(1)} fusion(bf16[640,4096]{1,0:T(8,128)(2,1)} %reshape_reshape.12, bf16[1,4096,1536]{2,1,0:T(8,128)(2,1)} %param.12), kind=kOutput, calls=%fused_computation.3 | convolution fusion | flops 8053063680 | bytes 21757952 | tf_op jit(solution)/shard_map/dot_general | solution.py:362
  109.7 0.0 copy-start.7
  109.7 1.9 copy-done.7
  111.6 0.0 slice-done.2
  111.6 0.0 slice-done.3
  111.6 6.1 %convolution_convert_fusion = bf16[640,4096]{1,0:T(8,128)(2,1)} fusion(bf16[1,768,4096]{2,1,0:T(8,128)(2,1)S(1)} %bitcast.49, f32[640,1536]{1,0:T(8,128)S(1)} %fusion.2), kind=kOutput, calls=%fused_computation.7 | convolution fusion | flops 4032102400 | bytes 15466496 | tf_op jit(solution)/shard_map/dot_general | solution.py:368
  117.7 8.9 %reshape_reshape.13 = bf16[128,160,128]{2,1,0:T(8,128)(2,1)} reshape(bf16[640,4096]{1,0:T(8,128)(2,1)} %convolution_convert_fusion) | data formatting | bytes 10485760 | tf_op jit(solution)/shard_map/reshape;reshape | solution.py:369
  126.6 25.4 %all-to-all-done.2 = bf16[128,160,128]{2,1,0:T(8,128)(2,1)} async-done(((bf16[128,160,128]{2,1,0:T(8,128)(2,1)}), bf16[128,160,128]{2,1,0:T(8,128)(2,1)}, u32[]{:S(2)}, u32[]{:S(2)}) %all-to-all-start.2) | async-done | bytes 5242912 | tf_op jit(solution)/shard_map/all_to_all | solution.py:295
  152.1 5.6 %all-to-all-start.1 = ((bf16[128,160,128]{2,1,0:T(8,128)(2,1)}), bf16[128,160,128]{2,1,0:T(8,128)(2,1)}, u32[]{:S(2)}, u32[]{:S(2)}) async-start(bf16[128,160,128]{2,1,0:T(8,128)(2,1)} %reshape_reshape.13), calls=%async_computation.1 | async-start | bytes 10485760 | tf_op jit(solution)/shard_map/all_to_all | solution.py:295
  157.7 0.0 slice-start
  157.7 8.9 %reshape_reshape.14 = bf16[640,4096]{1,0:T(8,128)(2,1)} reshape(bf16[128,160,128]{2,1,0:T(8,128)(2,1)} %all-to-all-done.2) | data formatting | bytes 10485760 | tf_op jit(solution)/shard_map/reshape;reshape | solution.py:358
  166.6 10.3 %multiply_convert_fusion.1 = (bf16[640,768]{1,0:T(8,128)(2,1)S(1)}, bf16[640,768]{1,0:T(8,128)(2,1)S(1)}) fusion(f32[640,1536]{1,0:T(8,128)} %copy-done.7, bf16[640,4096]{1,0:T(8,128)(2,1)} %reshape_reshape.14, bf16[1,768,4096]{2,1,0:T(8,128)(2,1)} %param.13), kind=kOutput, calls=%fused_computation.16 | convolution fusion | flops 4032921600 | bytes 17432576 | tf_op jit(solution)/shard_map/dot_general | solution.py:291
  176.9 0.0 slice-done
  176.9 0.0 slice-done.1
  176.9 0.0 copy-start.3
  177.0 17.5 %multiply_reduce_fusion = (f32[4096]{0:T(1024)S(1)}, bf16[640,4096]{1,0:T(8,128)(2,1)}) fusion(bf16[640,4096]{1,0:T(8,128)(2,1)S(1)} %bitcast.40, bf16[1,4096,1536]{2,1,0:T(8,128)(2,1)} %param.12, bf16[640,768]{1,0:T(8,128)(2,1)S(1)} %get-tuple-element.19, bf16[640,768]{1,0:T(8,128)(2,1)S(1)} %get-tuple-element.18), kind=kOutput, calls=%fused_computation.5 | convolution fusion | flops 8070098944 | bytes 25051136 | tf_op jit(solution)/shard_map/dot_general | solution.py:291
  194.4 0.0 copy-done.3
  194.5 0.1 reshape.47
  194.6 0.1 reshape.49
  194.7 0.1 reshape.45
  194.8 0.1 maximum_bitcast_fusion
  194.9 0.1 copy.16
  195.0 9.3 %reshape_reshape.15 = bf16[128,80,2,128]{3,2,1,0:T(2,128)(2,1)} reshape(bf16[640,4096]{1,0:T(8,128)(2,1)} %get-tuple-element.24) | data formatting | bytes 10485760 | tf_op jit(solution)/shard_map/reshape;reshape | solution.py:385
  204.3 7.0 %fusion.10 = bf16[128,81,2,128]{3,2,1,0:T(2,128)(2,1)} fusion(bf16[128,1,1,96]{3,2,1,0:T(2,128)(2,1)S(1)} %copy.16, bf16[128,80,2,128]{3,2,1,0:T(2,128)(2,1)} %reshape_reshape.15), kind=kLoop, calls=%fused_computation.11 | loop fusion | flops 15925248 | bytes 10575872 | tf_op jit(solution)/shard_map/concatenate | solution.py:386
  211.3 10.3 %all-to-all-done.1 = bf16[128,160,128]{2,1,0:T(8,128)(2,1)} async-done(((bf16[128,160,128]{2,1,0:T(8,128)(2,1)}), bf16[128,160,128]{2,1,0:T(8,128)(2,1)}, u32[]{:S(2)}, u32[]{:S(2)}) %all-to-all-start.1) | async-done | bytes 5242912 | tf_op jit(solution)/shard_map/all_to_all | solution.py:295
  221.6 5.6 %all-to-all-start.3 = ((bf16[128,81,2,128]{3,2,1,0:T(2,128)(2,1)}), bf16[128,81,2,128]{3,2,1,0:T(2,128)(2,1)}, u32[]{:S(2)}, u32[]{:S(2)}) async-start(bf16[128,81,2,128]{3,2,1,0:T(2,128)(2,1)} %fusion.10), calls=%async_computation.3 | async-start | bytes 10616832 | tf_op jit(solution)/shard_map/all_to_all | solution.py:295
  227.2 0.0 copy-start.4
  227.2 0.0 copy-done.1
  227.3 9.6 %outputs.1 = (bf16[128,4096]{1,0:T(8,128)(2,1)}, f32[4,128]{1,0:T(4,128)}) custom-call(s32[4,128]{1,0:T(4,128)S(1)} %copy-done.5, f32[4,128]{1,0:T(4,128)S(1)} %bitcast.38, bf16[128,4096]{1,0:T(8,128)(2,1)S(1)} %copy-done.1, bf16[128,4096]{1,0:T(8,128)(2,1)S(1)} %copy-done.2, bf16[20480,128]{1,0:T(8,128)(2,1)} %bitcast.5.returned), custom_call_target="tpu_custom_call" | custom-call | tf_op jit(solution)/shard_map/outputs/pallas_call | solution.py:389
  236.8 55.0 %all-to-all-done.3.returned = bf16[128,81,2,128]{3,2,1,0:T(2,128)(2,1)} async-done(((bf16[128,81,2,128]{3,2,1,0:T(2,128)(2,1)}), bf16[128,81,2,128]{3,2,1,0:T(2,128)(2,1)}, u32[]{:S(2)}, u32[]{:S(2)}) %all-to-all-start.3) | async-done | bytes 5308448 | tf_op jit(solution)/shard_map/all_to_all | solution.py:295
  291.8 0.0 copy-done.4
  291.8 6.3 %input_grad.1 = (bf16[128,4096]{1,0:T(8,128)(2,1)}, f32[1,32]{1,0:T(1,128)}) custom-call(s32[4,128]{1,0:T(4,128)S(1)} %copy-done.5, bf16[128,4096]{1,0:T(8,128)(2,1)S(1)} %copy-done.1, f32[128,128]{1,0:T(8,128)S(1)} %copy-done.4, f32[32,128]{1,0:T(8,128)S(1)} %bitcast.36, bf16[128,4096]{1,0:T(8,128)(2,1)S(1)} %copy-done.2, ...), custom_call_target="tpu_custom_call" | custom-call | tf_op jit(solution)/shard_map/input_grad/pallas_call | solution.py:402
  (8 shorter events, 0.1 us)
Async XLA Ops:
  6.8 12.0 %copy-start.2 = (bf16[128,4096]{1,0:T(8,128)(2,1)S(1)}, bf16[128,4096]{1,0:T(8,128)(2,1)}, u32[]{:S(2)}) copy-start(bf16[128,4096]{1,0:T(8,128)(2,1)} %grad.1) | copy-start | bytes 3145732
  6.8 11.9 %copy-start.5 = (s32[4,128]{1,0:T(4,128)S(1)}, s32[4,128]{1,0:T(4,128)}, u32[]{:S(2)}) copy-start(s32[4,128]{1,0:T(4,128)} %get-tuple-element.11.place.place_in) | copy-start | bytes 6148
  6.9 11.9 %copy-start.6 = (f32[128,4]{0,1:T(4,128)S(1)}, f32[128,4]{0,1:T(4,128)}, u32[]{:S(2)}) copy-start(f32[128,4]{0,1:T(4,128)} %param.10) | copy-start | bytes 6148
  6.9 75.7 %all-to-all-start = ((bf16[128,160,128]{2,1,0:T(8,128)(2,1)}), bf16[128,160,128]{2,1,0:T(8,128)(2,1)}, u32[]{:S(2)}, u32[]{:S(2)}) async-start(bf16[128,160,128]{2,1,0:T(8,128)(2,1)} %get-tuple-element.12), calls=%async_computation | async-start | bytes 10485760 | tf_op jit(solution)/shard_map/all_to_all | solution.py:295
  23.7 2.4 copy-start
  82.5 69.5 %all-to-all-start.2 = ((bf16[128,160,128]{2,1,0:T(8,128)(2,1)}), bf16[128,160,128]{2,1,0:T(8,128)(2,1)}, u32[]{:S(2)}, u32[]{:S(2)}) async-start(bf16[128,160,128]{2,1,0:T(8,128)(2,1)} %bitcast.34), calls=%async_computation.2 | async-start | bytes 10485760 | tf_op jit(solution)/shard_map/all_to_all | solution.py:295
  88.2 23.4 %slice-start.2 = ((s8[6291456]{0:T(1024)(128)(4,1)}), s8[2097152]{0:T(1024)(128)(4,1)S(1)}, s32[]{:S(2)}) async-start(s8[6291456]{0:T(1024)(128)(4,1)} %bitcast.48), calls=%async_computation.6 | async-start | bytes 4194304
  97.2 14.4 %slice-start.3 = ((s8[6291456]{0:T(1024)(128)(4,1)}), s8[4194304]{0:T(1024)(128)(4,1)S(1)}, s32[]{:S(2)}) async-start(s8[6291456]{0:T(1024)(128)(4,1)} %bitcast.48), calls=%async_computation.7 | async-start | bytes 8388608
  109.7 1.9 copy-start.7
  152.1 69.5 %all-to-all-start.1 = ((bf16[128,160,128]{2,1,0:T(8,128)(2,1)}), bf16[128,160,128]{2,1,0:T(8,128)(2,1)}, u32[]{:S(2)}, u32[]{:S(2)}) async-start(bf16[128,160,128]{2,1,0:T(8,128)(2,1)} %reshape_reshape.13), calls=%async_computation.1 | async-start | bytes 10485760 | tf_op jit(solution)/shard_map/all_to_all | solution.py:295
  157.7 19.2 %slice-start = ((s8[5242880]{0:T(1024)(128)(4,1)}), s8[1048576]{0:T(1024)(128)(4,1)S(1)}, s32[]{:S(2)}) async-start(s8[5242880]{0:T(1024)(128)(4,1)} %bitcast.39), calls=%async_computation.4 | async-start | bytes 2097152
  166.6 10.3 %slice-start.1 = ((s8[5242880]{0:T(1024)(128)(4,1)}), s8[4194304]{0:T(1024)(128)(4,1)S(1)}, s32[]{:S(2)}) async-start(s8[5242880]{0:T(1024)(128)(4,1)} %bitcast.39), calls=%async_computation.5 | async-start | bytes 8388608
  176.9 17.5 %copy-start.3 = (f32[4096]{0:T(1024)S(1)}, f32[4096]{0:T(1024)}, u32[]{:S(2)}) copy-start(f32[4096]{0:T(1024)} %param.8) | copy-start | bytes 49156
  211.3 15.9 %copy-start.1 = (bf16[128,4096]{1,0:T(8,128)(2,1)S(1)}, bf16[128,4096]{1,0:T(8,128)(2,1)}, u32[]{:S(2)}) copy-start(bf16[128,4096]{1,0:T(8,128)(2,1)} %x.3) | copy-start | bytes 3145732
  221.6 70.2 %all-to-all-start.3 = ((bf16[128,81,2,128]{3,2,1,0:T(2,128)(2,1)}), bf16[128,81,2,128]{3,2,1,0:T(2,128)(2,1)}, u32[]{:S(2)}, u32[]{:S(2)}) async-start(bf16[128,81,2,128]{3,2,1,0:T(2,128)(2,1)} %fusion.10), calls=%async_computation.3 | async-start | bytes 10616832 | tf_op jit(solution)/shard_map/all_to_all | solution.py:295
  227.2 64.6 %copy-start.4 = (f32[128,128]{1,0:T(8,128)S(1)}, f32[128,128]{1,0:T(8,128)}, u32[]{:S(2)}) copy-start(f32[128,128]{1,0:T(8,128)} %get-tuple-element.14.inverse) | copy-start | bytes 196612
